TPU v7x, 512 devices: a whole 4x8x8 slice. The times are simulated.
512 devices in a mesh: pair: 16 (over z, core), virt: 32 (over x, y).
Axes of the slice: x: 4, y: 8, z: 8, core: 2. Of those that a mesh axis runs over, the one named last changes fastest.
Arguments:
- lam: bfloat16 [16, 16, 256, 256], P('pair', None, 'virt'), may hold values from -4 to 4
- drive: float32 [16, 16, 256, 256], P('pair', None, 'virt'), may hold values from -45 to 45
- order: int32 [16, 16], P('pair'), may hold values from 0 to 15, each once within a row
- dom_tiles: int32 [16, 16, 2], P('pair'), may hold values from 0 to 31, as said below
- dom_len: int32 [16, 16], P('pair'), may hold values from 1 to 2, as said below
- factors: bfloat16 [32, 4, 128, 128], P('virt'), may hold values from -0.5 to 0.5
- e_occ: float32 [16], replicated, may hold values from -1.2 to -0.4
- e_virt: bfloat16 [32, 128], P('virt'), may hold values from 0.19921875 to 3
Outputs:
- lam_next: bfloat16 [16, 16, 256, 256], P('pair', None, 'virt')
- res_norm: float32 [2, 16, 16], P(None, 'pair')
Inputs may be any that keep to these rules, and one draw needn't show every extreme that they name: Each row is a permutation; order[i, s] = j puts the pair (i, j) in slot s of row i. dom_tiles[i, j] = dom_tiles[j, i]; the tiles of one pair are distinct. dom_len[i, j] = dom_len[j, i]; every pair (i, i) has all 2 tiles live.
All inputs are finite; a program needn't handle non-finite values.
Results may differ from a plain program's by a relative error of at most 0.0054.
Values may be sent and summed in bfloat16 or wider, within the bound.
A program may use at most 64 MiB of HBM per device.

v0:
```python
from functools import partial

import jax
import jax.numpy as jnp
from jax import lax
from jax.sharding import PartitionSpec as P

ITERS = 2


def right_half(items, table, row_count, tile_width):
    block, tile_ids = items
    pair_factors = jnp.take(table, tile_ids, axis=0)
    domain_tiles = tile_ids.shape[0]
    block_three = block.reshape(row_count, domain_tiles, tile_width)
    result = jnp.einsum(
        "lqbd,rld->qrlb", pair_factors, block_three, preferred_element_type=jnp.float32
    )
    return result.astype(jnp.bfloat16).reshape(
        pair_factors.shape[1], row_count, domain_tiles * tile_width
    )


def left_half(items, table, tile_width):
    received, tile_ids = items
    pair_factors = jnp.take(table, tile_ids, axis=0)
    domain_tiles = tile_ids.shape[0]
    col_count = received.shape[2]
    received_four = received.reshape(received.shape[0], domain_tiles, tile_width, col_count)
    result = jnp.einsum(
        "kqac,qkcr->kar", pair_factors, received_four, preferred_element_type=jnp.float32
    )
    return result.astype(jnp.bfloat16).reshape(domain_tiles * tile_width, col_count)


def shards(lam, drive, order, dom_tiles, dom_len, factors, e_occ, e_virt):
    table, energies = (
        lax.all_gather(factors, "virt", axis=0, tiled=True),
        lax.all_gather(e_virt, "virt", axis=0, tiled=True),
    )
    tile_width = factors.shape[2]
    order_row = order[0]
    pair_count = order_row.shape[0]
    row_count = lam.shape[2]
    dom_width = lam.shape[3]
    slot_ids = jnp.arange(pair_count, dtype=jnp.int32)
    onehot = (order_row[:, None] == slot_ids[None, :]).astype(jnp.int32)
    slot_of = jnp.sum(onehot * slot_ids[:, None], axis=0)
    dom_slot = jnp.take(dom_tiles[0], order_row, axis=0)
    len_slot = jnp.take(dom_len[0], order_row, axis=0)
    first_row = lax.axis_index("virt") * row_count
    col_tile = jnp.arange(dom_width, dtype=jnp.int32) // tile_width
    row_tile = (first_row + jnp.arange(row_count, dtype=jnp.int32)) // tile_width
    live_cols = col_tile[None, :] < len_slot[:, None]
    live_rows = row_tile[None, :] < len_slot[:, None]
    live_mask = live_rows[:, :, None] & live_cols[:, None, :]
    col_energy = (
        jnp.take(energies, dom_slot, axis=0).astype(jnp.float32).reshape(pair_count, dom_width)
    )
    row_energy = lax.dynamic_slice_in_dim(col_energy, first_row, row_count, 1)
    occ_sum = e_occ[lax.axis_index("pair")] + jnp.take(e_occ, order_row)
    denominator = row_energy[:, :, None] + col_energy[:, None, :] - occ_sum[:, None, None]
    source = drive[0]
    current = jnp.where(live_mask, lam[0], jnp.zeros_like(lam[0]))
    count = (len_slot * tile_width).astype(jnp.float32) ** 2
    right_fn = partial(right_half, table=table, row_count=row_count, tile_width=tile_width)
    left_fn = partial(left_half, table=table, tile_width=tile_width)
    norm_list = []
    for step in range(ITERS):
        flipped = jnp.swapaxes(current, 1, 2)
        moved_rows = lax.all_to_all(flipped, "virt", split_axis=1, concat_axis=2, tiled=True)
        partner = lax.all_to_all(
            jnp.take(moved_rows, slot_of, axis=0), "pair", split_axis=0, concat_axis=0, tiled=True
        )
        partner = jnp.take(partner, order_row, axis=0)
        summed = (current.astype(jnp.float32) + partner.astype(jnp.float32)).astype(jnp.bfloat16)
        half_prod = lax.map(right_fn, (summed, dom_slot))
        half_prod = lax.all_to_all(half_prod, "virt", split_axis=3, concat_axis=2, tiled=True)
        ladder_cols = lax.map(left_fn, (half_prod, dom_slot))
        ladder = lax.all_to_all(
            ladder_cols, "virt", split_axis=1, concat_axis=2, tiled=True
        ).astype(jnp.float32)
        target = source + ladder
        resid = jnp.where(
            live_mask, target - denominator * current.astype(jnp.float32), jnp.float32(0.0)
        )
        current = jnp.where(live_mask, target / denominator, jnp.float32(0.0)).astype(jnp.bfloat16)
        square_sums = jnp.sum(resid * resid, axis=(1, 2))
        totals = lax.psum(square_sums, "virt")
        norm_list.append(jnp.sqrt(totals / count + 1e-06))
    norms = jnp.stack(norm_list)
    return (current[None], norms[:, None, :])


def solution(mesh):
    return jax.shard_map(
        shards,
        mesh=mesh,
        in_specs=(
            P("pair", None, "virt", None),
            P("pair", None, "virt", None),
            P("pair", None),
            P("pair", None, None),
            P("pair", None),
            P("virt", None, None, None),
            P(),
            P("virt", None),
        ),
        out_specs=(P("pair", None, "virt", None), P(None, "pair", None)),
        check_vma=False,
    )
```

profile of v0, /device:TPU:8, one launch (start us, length us, event | category | flops | bytes accessed | tf_op | source)
XLA Modules:
  0.0 532.3 jit_solution(9029052951986028170)
XLA Ops:
  12.7 10.2 %all-to-all-start = ((bf16[32,2,512]{2,1,0:T(2,128)(2,1)}), bf16[32,2,512]{2,1,0:T(2,128)(2,1)S(1)}, u32[]{:S(2)}, u32[]{:S(2)}) async-start(bf16[32,2,512]{2,1,0:T(2,128)(2,1)} %reshape.422), calls=%async_computation | async-start | bytes 131072 | tf_op jit(solution)/shard_map/all_to_all | solution.py:71
  23.7 8.3 %all-to-all-done = bf16[32,2,512]{2,1,0:T(2,128)(2,1)S(1)} async-done(((bf16[32,2,512]{2,1,0:T(2,128)(2,1)}), bf16[32,2,512]{2,1,0:T(2,128)(2,1)S(1)}, u32[]{:S(2)}, u32[]{:S(2)}) %all-to-all-start) | async-done | bytes 65568 | tf_op jit(solution)/shard_map/all_to_all | solution.py:71
  34.0 10.5 %all-to-all-start.1 = ((bf16[16,8,256]{2,1,0:T(8,128)(2,1)}), bf16[16,8,256]{2,1,0:T(8,128)(2,1)S(1)}, u32[]{:S(2)}, u32[]{:S(2)}) async-start(bf16[16,8,256]{2,1,0:T(8,128)(2,1)} %broadcast_select_fusion.1), calls=%async_computation.1 | async-start | bytes 131072 | tf_op jit(solution)/shard_map/all_to_all | solution.py:72
  44.6 7.7 %all-to-all-done.1 = bf16[16,8,256]{2,1,0:T(8,128)(2,1)S(1)} async-done(((bf16[16,8,256]{2,1,0:T(8,128)(2,1)}), bf16[16,8,256]{2,1,0:T(8,128)(2,1)S(1)}, u32[]{:S(2)}, u32[]{:S(2)}) %all-to-all-start.1) | async-done | bytes 65568 | tf_op jit(solution)/shard_map/all_to_all | solution.py:72
  53.0 50.0 %all-gather.3.cloned.1.call-done = bf16[32,4,128,128]{3,2,1,0:T(8,128)(2,1)} async-done(((bf16[1,4,128,128]{3,2,1,0:T(8,128)(2,1)}), bf16[32,4,128,128]{3,2,1,0:T(8,128)(2,1)}) %all-gather.3.cloned.1.call-update) | async-done | bytes 4194320 | tf_op jit(solution)/shard_map/all_gather | solution.py:38
  103.1 49.3 %while.40 = (s32[]{:T(128)}, bf16[16,4,8,256]{3,2,1,0:T(8,128)(2,1)S(1)}, bf16[16,8,256]{2,1,0:T(8,128)(2,1)S(1)}, s32[16,2]{1,0:T(8,128)S(1)}, bf16[32,4,128,128]{3,2,1,0:T(8,128)(2,1)}, /*index=5*/s32[]{:T(128)}) while((s32[]{:T(128)}, bf16[16,4,8,256]{3,2,1,0:T(8,128)(2,1)S(1)}, bf16[16,8,256]{2,1,0:T(8,128)(2,1)S(1)}, ...), condition=%wide.region_2.0_spmd, body=%wide.region_1.4_spmd.sunk | while | flops 2237454 | bytes 844403 | solution.py:77
  109.3 2.8 gather_fusion
  124.7 2.8 gather_fusion
  140.1 2.8 gather_fusion
  152.4 2.9 copy.244
  155.4 2.9 reshape.424
  158.3 5.8 %all-to-all-start.2 = ((bf16[32,2,2048]{2,1,0:T(2,128)(2,1)}), bf16[32,2,2048]{2,1,0:T(2,128)(2,1)S(1)}, u32[]{:S(2)}, u32[]{:S(2)}) async-start(bf16[32,2,2048]{2,1,0:T(2,128)(2,1)} %reshape.424), calls=%async_computation.2 | async-start | bytes 524288 | tf_op jit(solution)/shard_map/all_to_all | solution.py:78
  164.3 35.5 %all-gather = bf16[32,1,128]{2,1,0:T(2,128)(2,1)S(1)} all-gather(bf16[1,1,128]{2,1,0:T(2,128)(2,1)S(1)} %bitcast.238), channel_id=1, replica_groups=mesh['pair'=16,'virt'=32] {'virt'}, dimensions={0}, use_global_device_ids=true | all-gather | bytes 8448 | tf_op jit(solution)/shard_map/all_gather | solution.py:39
  208.8 49.3 %while.41 = (s32[]{:T(128)}, bf16[16,256,8]{1,2,0:T(8,128)(2,1)S(1)}, s32[16,2]{1,0:T(8,128)S(1)}, bf16[32,4,128,128]{3,2,1,0:T(8,128)(2,1)}, bf16[16,4,256,8]{2,3,1,0:T(8,128)(2,1)S(1)}, /*index=5*/s32[]{:T(128)}) while((s32[]{:T(128)}, bf16[16,256,8]{1,2,0:T(8,128)(2,1)S(1)}, s32[16,2]{1,0:T(8,128)S(1)}, ...), condition=%wide.region_4.7_spmd, body=%wide.region_3.6_spmd.sunk | while | flops 2231310 | bytes 812651 | solution.py:79
  218.0 2.8 gather_fusion.1
  242.7 2.8 gather_fusion.1
  251.9 2.8 gather_fusion.1
  259.6 6.9 %all-to-all-start.3 = ((bf16[32,2,512]{2,1,0:T(2,128)(2,1)}), bf16[32,2,512]{2,1,0:T(2,128)(2,1)S(1)}, u32[]{:S(2)}, u32[]{:S(2)}) async-start(bf16[32,2,512]{2,1,0:T(2,128)(2,1)} %reshape.426), calls=%async_computation.3 | async-start | bytes 131072 | tf_op jit(solution)/shard_map/all_to_all | solution.py:80
  267.2 8.4 %all-to-all-done.3 = bf16[32,2,512]{2,1,0:T(2,128)(2,1)S(1)} async-done(((bf16[32,2,512]{2,1,0:T(2,128)(2,1)}), bf16[32,2,512]{2,1,0:T(2,128)(2,1)S(1)}, u32[]{:S(2)}, u32[]{:S(2)}) %all-to-all-start.3) | async-done | bytes 65568 | tf_op jit(solution)/shard_map/all_to_all | solution.py:80
  277.5 13.1 %all_to_all.100 = bf16[32,2,512]{2,1,0:T(2,128)(2,1)S(1)} all-to-all(bf16[32,2,512]{2,1,0:T(2,128)(2,1)S(1)} %reshape.428), channel_id=1, replica_groups=mesh['pair'=16,'virt'=32] {'virt'}, dimensions={0} | all-to-all | bytes 131072 | tf_op jit(solution)/shard_map/all_to_all | solution.py:71
  292.6 7.5 %all-to-all-start.5 = ((bf16[16,8,256]{2,1,0:T(8,128)(2,1)}), bf16[16,8,256]{2,1,0:T(8,128)(2,1)S(1)}, u32[]{:S(2)}, u32[]{:S(2)}) async-start(bf16[16,8,256]{2,1,0:T(8,128)(2,1)} %broadcast_select_fusion), calls=%async_computation.5 | async-start | bytes 131072 | tf_op jit(solution)/shard_map/all_to_all | solution.py:72
  300.1 7.9 %all-to-all-done.5 = bf16[16,8,256]{2,1,0:T(8,128)(2,1)S(1)} async-done(((bf16[16,8,256]{2,1,0:T(8,128)(2,1)}), bf16[16,8,256]{2,1,0:T(8,128)(2,1)S(1)}, u32[]{:S(2)}, u32[]{:S(2)}) %all-to-all-start.5) | async-done | bytes 65568 | tf_op jit(solution)/shard_map/all_to_all | solution.py:72
  308.6 49.3 %while.42 = (s32[]{:T(128)}, bf16[16,4,8,256]{3,2,1,0:T(8,128)(2,1)S(1)}, bf16[16,8,256]{2,1,0:T(8,128)(2,1)S(1)}, s32[16,2]{1,0:T(8,128)S(1)}, bf16[32,4,128,128]{3,2,1,0:T(8,128)(2,1)}, /*index=5*/s32[]{:T(128)}) while((s32[]{:T(128)}, bf16[16,4,8,256]{3,2,1,0:T(8,128)(2,1)S(1)}, bf16[16,8,256]{2,1,0:T(8,128)(2,1)S(1)}, ...), condition=%wide.region_6.9_spmd, body=%wide.region_5.8_spmd.sunk | while | flops 2237454 | bytes 844403 | solution.py:77
  308.7 2.8 gather_fusion.2
  324.1 2.8 gather_fusion.2
  339.5 2.8 gather_fusion.2
  358.0 3.0 copy.256
  363.3 17.0 %all_to_all.101 = bf16[32,2,2048]{2,1,0:T(2,128)(2,1)S(1)} all-to-all(bf16[32,2,2048]{2,1,0:T(2,128)(2,1)S(1)} %reshape.430), channel_id=1, replica_groups=mesh['pair'=16,'virt'=32] {'virt'}, dimensions={0} | all-to-all | bytes 524288 | tf_op jit(solution)/shard_map/all_to_all | solution.py:78
  387.1 49.3 %while.43 = (s32[]{:T(128)}, bf16[16,256,8]{1,2,0:T(8,128)(2,1)S(1)}, s32[16,2]{1,0:T(8,128)S(1)}, bf16[32,4,128,128]{3,2,1,0:T(8,128)(2,1)}, bf16[16,4,256,8]{2,3,1,0:T(8,128)(2,1)S(1)}, /*index=5*/s32[]{:T(128)}) while((s32[]{:T(128)}, bf16[16,256,8]{1,2,0:T(8,128)(2,1)S(1)}, s32[16,2]{1,0:T(8,128)S(1)}, ...), condition=%wide.region_8.11_spmd, body=%wide.region_7.10_spmd.sunk | while | flops 2231310 | bytes 812651 | solution.py:79
  438.0 4.6 all-to-all-start.7
  443.2 8.4 %all-to-all-done.7 = bf16[32,2,512]{2,1,0:T(2,128)(2,1)S(1)} async-done(((bf16[32,2,512]{2,1,0:T(2,128)(2,1)}), bf16[32,2,512]{2,1,0:T(2,128)(2,1)S(1)}, u32[]{:S(2)}, u32[]{:S(2)}) %all-to-all-start.7) | async-done | bytes 65568 | tf_op jit(solution)/shard_map/all_to_all | solution.py:80
  454.1 70.7 %all-reduce = (f32[16]{0:T(128)S(1)}, f32[16]{0:T(128)S(1)}) all-reduce(f32[16]{0:T(128)S(1)} %get-tuple-element.203, f32[16]{0:T(128)S(1)} %get-tuple-element.202), channel_id=1, replica_groups=mesh['pair'=16,'virt'=32] {'virt'}, use_global_device_ids=true, to_apply=%region_12.15 | all-reduce | flops 32 | bytes 256 | tf_op jit(solution)/shard_map/psum | solution.py:89
  (376 shorter events, 209.7 us)
Async XLA Ops:
  7.2 1.4 copy-start
  7.2 15.7 %copy-start.5 = (s32[1,16]{1,0:T(1,128)S(1)}, s32[1,16]{1,0:T(1,128)}, u32[]{:S(2)}) copy-start(s32[1,16]{1,0:T(1,128)} %param.22) | copy-start | bytes 196
  7.2 15.8 %copy-start.4 = (s32[1,16,2]{1,2,0:T(2,128)S(1)}, s32[1,16,2]{1,2,0:T(2,128)}, u32[]{:S(2)}) copy-start(s32[1,16,2]{1,2,0:T(2,128)} %param.23) | copy-start | bytes 388
  7.2 95.8 %all-gather.3.cloned.1.call-start = ((), (), s32[]{:S(2)}) async-start(), calls=%async_computation.8 | async-start | bytes 4325376 | tf_op jit(solution)/shard_map/all_gather | solution.py:38
  11.1 41.8 %copy-start.3 = (bf16[1,16,8,256]{3,2,1,0:T(8,128)(2,1)S(1)}, bf16[1,16,8,256]{3,2,1,0:T(8,128)(2,1)}, u32[]{:S(2)}) copy-start(bf16[1,16,8,256]{3,2,1,0:T(8,128)(2,1)} %param.20) | copy-start | bytes 196612
  12.7 19.3 %all-to-all-start = ((bf16[32,2,512]{2,1,0:T(2,128)(2,1)}), bf16[32,2,512]{2,1,0:T(2,128)(2,1)S(1)}, u32[]{:S(2)}, u32[]{:S(2)}) async-start(bf16[32,2,512]{2,1,0:T(2,128)(2,1)} %reshape.422), calls=%async_computation | async-start | bytes 131072 | tf_op jit(solution)/shard_map/all_to_all | solution.py:71
  34.0 18.4 %all-to-all-start.1 = ((bf16[16,8,256]{2,1,0:T(8,128)(2,1)}), bf16[16,8,256]{2,1,0:T(8,128)(2,1)S(1)}, u32[]{:S(2)}, u32[]{:S(2)}) async-start(bf16[16,8,256]{2,1,0:T(8,128)(2,1)} %broadcast_select_fusion.1), calls=%async_computation.1 | async-start | bytes 131072 | tf_op jit(solution)/shard_map/all_to_all | solution.py:72
  152.4 11.9 %copy-start.6 = (bf16[1,128]{1,0:T(2,128)(2,1)S(1)}, bf16[1,128]{1,0:T(2,128)(2,1)}, u32[]{:S(2)}) copy-start(bf16[1,128]{1,0:T(2,128)(2,1)} %param.27) | copy-start | bytes 772
  152.4 47.5 %copy-start.1 = (f32[16]{0:T(128)S(1)}, f32[16]{0:T(128)}, u32[]{:S(2)}) copy-start(f32[16]{0:T(128)} %param.26) | copy-start | bytes 196
  158.3 43.6 %all-to-all-start.2 = ((bf16[32,2,2048]{2,1,0:T(2,128)(2,1)}), bf16[32,2,2048]{2,1,0:T(2,128)(2,1)S(1)}, u32[]{:S(2)}, u32[]{:S(2)}) async-start(bf16[32,2,2048]{2,1,0:T(2,128)(2,1)} %reshape.424), calls=%async_computation.2 | async-start | bytes 524288 | tf_op jit(solution)/shard_map/all_to_all | solution.py:78
  258.4 18.0 %copy-start.2 = (f32[1,16,8,256]{3,2,1,0:T(8,128)S(1)}, f32[1,16,8,256]{3,2,1,0:T(8,128)}, u32[]{:S(2)}) copy-start(f32[1,16,8,256]{3,2,1,0:T(8,128)} %param.21) | copy-start | bytes 393220
  259.6 16.0 %all-to-all-start.3 = ((bf16[32,2,512]{2,1,0:T(2,128)(2,1)}), bf16[32,2,512]{2,1,0:T(2,128)(2,1)S(1)}, u32[]{:S(2)}, u32[]{:S(2)}) async-start(bf16[32,2,512]{2,1,0:T(2,128)(2,1)} %reshape.426), calls=%async_computation.3 | async-start | bytes 131072 | tf_op jit(solution)/shard_map/all_to_all | solution.py:80
  292.6 15.4 %all-to-all-start.5 = ((bf16[16,8,256]{2,1,0:T(8,128)(2,1)}), bf16[16,8,256]{2,1,0:T(8,128)(2,1)S(1)}, u32[]{:S(2)}, u32[]{:S(2)}) async-start(bf16[16,8,256]{2,1,0:T(8,128)(2,1)} %broadcast_select_fusion), calls=%async_computation.5 | async-start | bytes 131072 | tf_op jit(solution)/shard_map/all_to_all | solution.py:72
  438.0 13.7 %all-to-all-start.7 = ((bf16[32,2,512]{2,1,0:T(2,128)(2,1)}), bf16[32,2,512]{2,1,0:T(2,128)(2,1)S(1)}, u32[]{:S(2)}, u32[]{:S(2)}) async-start(bf16[32,2,512]{2,1,0:T(2,128)(2,1)} %reshape.432), calls=%async_computation.7 | async-start | bytes 131072 | tf_op jit(solution)/shard_map/all_to_all | solution.py:80
Sparse Core Ops, SparseCore 0:
  11.2 91.7 all-gather.2
where the time goes:
time: 535 us; the launch traced here: 532 us
  local copies, waits for them, and re-layouts  219 us (41%)
  blocking collectives  136 us (25%)
  waiting for transfers between devices  91.4 us (17%)
  starting transfers between devices  45.5 us (9%)
  matrix products  15.5 us (3%)
  between operations  14.5 us (3%)
  other arithmetic  8.34 us (2%)
    gather x32, local copies, waits for them, and re-layouts, right_half(): pair_factors = jnp.take(table, tile_ids, axis=0)  89.1 us
    gather x32, local copies, waits for them, and re-layouts, left_half(): pair_factors = jnp.take(table, tile_ids, axis=0)  89.1 us
    psum x1, blocking collectives, shards(): totals = lax.psum(square_sums, 'virt')  70.7 us
    all_gather x1, waiting for transfers between devices, shards(): lax.all_gather(factors, 'virt', axis=0, tiled=True)  50 us
    all_gather x1, blocking collectives, shards(): lax.all_gather(e_virt, 'virt', axis=0, tiled=True)  35.5 us
    all_to_all x2, starting transfers between devices, shards(): lax.all_to_all(jnp.take(moved_rows, slot_of, axis=0), 'pair', split_axis=...  18 us
    all_to_all x1, blocking collectives, shards(): lax.all_to_all(half_prod, 'virt', split_axis=3, concat_axis=2, tiled=True)  17 us
    all_to_all x2, waiting for transfers between devices, shards(): lax.all_to_all(ladder_cols, 'virt', split_axis=1, concat_axis=2, tiled=True)  16.8 us
  transfers between devices with their start and end apart: 7, of which 6 were waited for; matrix products, arithmetic and copies ran while one was open for 2% of the time, Pallas kernels for 0%

commit v1 on v0

v1 whole, which is shorter than its diff:
```python
import functools

import jax
import jax.numpy as jnp
from jax import lax
from jax.experimental import pallas as pl
from jax.experimental.pallas import tpu as pltpu
from jax.sharding import PartitionSpec as P

F32, BF16, I32 = jnp.float32, jnp.bfloat16, jnp.int32
MESH = pl.DeviceIdType.MESH
NZ, NV, NO, T = 8, 32, 16, 128


def host_of(z, c, d, cj, ty):
    if d == 0:
        diag = c == cj
        g = jnp.where(diag, 1, 0)
        t = jnp.where(diag, c, ty)
        return z, 2 * g + t, jnp.where(diag, ty, c)
    if d < 4:
        zh = lax.rem(z + (d >= 2), NZ) if d >= 2 else z
        return zh, 2 * (2 + 4 * (d - 1) + 2 * c + cj) + ty, 0
    if d > 4:
        e = NZ - d
        zh = lax.rem(z + d + (e >= 2), NZ)
        return zh, 2 * (2 + 4 * (e - 1) + 2 * cj + c) + ty, 1
    low = z < 4
    c_low, c_high = jnp.where(low, c, cj), jnp.where(low, cj, c)
    zh = lax.rem(lax.rem(z, 4) + 2 + 4 * c_low, NZ)
    return zh, 2 * (14 + c_high) + ty, jnp.where(low, 0, 1)


def pair_of(zh, v):
    g, t = lax.div(v, 2), lax.rem(v, 2)
    b = jnp.maximum(g - 2, 0)
    d = lax.div(b, 4) + 1
    z_mid = lax.rem(zh + NZ - jnp.where(d >= 2, 1, 0), NZ)
    i_mid = 2 * z_mid + lax.rem(lax.div(b, 2), 2)
    j_mid = 2 * lax.rem(z_mid + d, NZ) + lax.rem(b, 2)
    zl = lax.rem(zh + 6, NZ)
    z_far = lax.rem(zl, 4)
    i_far = 2 * z_far + lax.div(zl, 4)
    j_far = 2 * (z_far + 4) + (g - 14)
    i = jnp.where(g == 0, 2 * zh, jnp.where(g == 1, 2 * zh + t, jnp.where(g >= 14, i_far, i_mid)))
    j = jnp.where(g == 0, 2 * zh + 1, jnp.where(g == 1, 2 * zh + t, jnp.where(g >= 14, j_far, j_mid)))
    return i, j


def kernel(
    lam, drive, order, tiles, lens, factors, e_occ, e_virt,
    out, norms,
    send, recv, buf1, sel, buf2, ev_own, evb, tab_own, tab, tab_s, cur, drv, e_row, e_col, nacc, osend, orecv,
    s_amp, r_amp, s_fac, r_fac, s_ev, r_ev, s_tab, r_tab, s_sel, r_sel, s_out, r_out, l_sem,
):
    p, v = lax.axis_index("pair"), lax.axis_index("virt")
    z, c = lax.div(p, 2), lax.rem(p, 2)
    k_own = lax.div(v, 16)
    host = c == 1
    my_i, my_j = pair_of(z, v)
    my_t = lax.rem(v, 2)
    diag = lax.div(v, 2) == 1

    def remote(src, dst, ss, rs, pp, vv):
        return pltpu.make_async_remote_copy(
            src_ref=src, dst_ref=dst, send_sem=ss, recv_sem=rs,
            device_id={"pair": pp, "virt": vv}, device_id_type=MESH,
        )

    barrier = pltpu.get_barrier_semaphore()

    def greet(pp, vv):
        pl.semaphore_signal(barrier, inc=1, device_id={"pair": pp, "virt": vv}, device_id_type=MESH)

    targets = []
    for d in range(NZ):
        for cj in range(2):
            for h in range(2):
                zh, vh, side = host_of(z, c, d, cj, lax.rem(k_own + h, 2))
                own = jnp.logical_and(host, vh == v) if d < 2 else None
                targets.append((d, cj, h, 2 * zh + 1, vh, side, own))

    def away(own, act):
        if own is None:
            act()
        else:
            pl.when(jnp.logical_not(own))(act)

    @pl.when(host)
    def _():
        @pl.loop(1, NV)
        def _(d):
            greet(p, lax.rem(v + d, NV))

        @pl.loop(1, NO)
        def _(d):
            greet(lax.rem(p + d, NO), v)

        for s in range(2):
            row = my_i if s == 0 else jnp.where(diag, my_i, my_j)

            @pl.loop(0, NV)
            def _(w):
                self_home = jnp.logical_and(row == p, w == v)

                @pl.when(jnp.logical_not(self_home))
                def _():
                    greet(row, w)

    to_self = jnp.int32(0)
    for d, cj, h, pp, vv, side, own in targets:
        away(own, functools.partial(greet, pp, vv))
        if own is not None:
            to_self += own.astype(I32)

    def find(s, found):
        o = order[0, s]
        return tuple(
            jnp.where(o == 2 * lax.rem(z + n // 2, NZ) + n % 2, s, f) for n, f in enumerate(found)
        )

    slots = lax.fori_loop(0, NO, find, (jnp.int32(0),) * NO)
    for n in range(NO):
        own_lam = lam[0, slots[n]].astype(F32)
        own_drive = drive[0, slots[n]]
        for h in range(2):
            cols = slice(h * T, (h + 1) * T)
            send[n, h] = jnp.concatenate([own_lam[:, cols], own_drive[:, cols]], axis=0).astype(BF16)
    lane = lax.broadcasted_iota(I32, (1, T), 1)
    row_table = jnp.zeros((1, T), I32)
    for j in range(NO):
        for k in range(2):
            row_table = jnp.where(lane == 2 * j + k, tiles[0, j, k], row_table)
        row_table = jnp.where(lane == 32 + j, lens[0, j], row_table)
    tab_own[...] = row_table
    ev_own[...] = e_virt[...].astype(F32)

    pl.semaphore_wait(barrier, jnp.where(host, NV + 7 + NV - 1 + 2 * NV, NV + 8) - 2 * to_self)

    q_own, r_own = lax.div(z, 2), lax.rem(z, 2)

    def slice_copy(vv):
        return remote(
            factors.at[0, q_own, pl.ds(pl.multiple_of(64 * r_own, 64), 64)], buf1.at[v], s_fac, r_fac, p, vv
        )

    def ev_copy(vv):
        return remote(ev_own, evb.at[v], s_ev, r_ev, p, vv)

    def tab_copy(dz):
        return remote(tab_own, tab.at[p], s_tab, r_tab, 2 * lax.rem(z + dz, NZ) + 1, v)

    @pl.when(host)
    def _():
        @pl.loop(1, NV)
        def _(d):
            slice_copy(lax.rem(v + d, NV)).start()

        pltpu.make_async_copy(
            factors.at[0, q_own, pl.ds(pl.multiple_of(64 * r_own, 64), 64)], buf1.at[v], r_fac
        ).start()

        @pl.loop(1, NV)
        def _(d):
            ev_copy(lax.rem(v + d, NV)).start()

        pltpu.make_async_copy(ev_own, evb.at[v], r_ev).start()
        pltpu.make_async_copy(tab_own, tab.at[p], r_tab).start()

    @pl.when(jnp.logical_not(host))
    def _():
        tab_copy(0).start()

    for dz in range(1, NZ):
        tab_copy(dz).start()

    def amp_copy(n, h, side, pp, vv):
        return remote(send.at[n, h], recv.at[side, v], s_amp, r_amp, pp, vv)

    for d, cj, h, pp, vv, side, own in targets:
        n = 2 * d + cj
        away(own, lambda: amp_copy(n, h, side, pp, vv).start())
        if own is not None:
            @pl.when(own)
            def _():
                pltpu.make_async_copy(send.at[n, h], recv.at[side, v], r_amp).start()

    @pl.when(host)
    def _():
        pltpu.make_async_copy(tab, tab, r_tab).wait()
        to_smem = pltpu.make_async_copy(tab, tab_s, l_sem)
        to_smem.start()
        to_smem.wait()
        pltpu.make_async_copy(buf1, buf1, r_fac).wait()
        for dz in range(1, NZ):
            zd = lax.rem(z + dz, NZ)
            i, j = pair_of(zd, v)
            for k in range(2):
                sel[dz, k] = buf1[tab_s[i, 0, 2 * j + k]]
            remote(sel.at[dz], buf2.at[:, z], s_sel, r_sel, 2 * zd + 1, v).start()
        own_tiles = [tab_s[my_i, 0, 2 * my_j + k] for k in range(2)]
        for k in range(2):
            sel[0, k] = buf1[own_tiles[k]]
        pltpu.make_async_copy(sel.at[0], buf2.at[:, z], r_sel).start()
        length = tab_s[my_i, 0, 32 + my_j]
        occ = e_occ[my_i] + e_occ[my_j]
        pltpu.make_async_copy(evb, evb, r_ev).wait()
        for k in range(2):
            energy = evb[own_tiles[k]]
            e_row[k] = energy
            e_col[k] = jnp.transpose(jnp.broadcast_to(energy, (T, T)))
        pltpu.make_async_copy(recv, recv, r_amp).wait()
        for s in range(2):
            pieces = recv[s].astype(F32).reshape(NV, 2, 8, T)
            cur[s] = pieces[:, 0].reshape(2, T, T)
            drv[s] = pieces[:, 1].reshape(2, T, T)
        for s in range(2):
            for k in range(2):
                crossed = jnp.where(diag, s, my_t) == 1
                l = jnp.where(crossed, 1 - k, k)
                live = jnp.logical_and(k < length, l < length)
                cur[s, k] = jnp.where(live, cur[s, k], 0.0)

        pltpu.make_async_copy(buf2, buf2, r_sel).wait()

        def block_step(it, ps, pk, qs, qk, l, partner_counts):
            mine, theirs = cur[ps, pk], cur[qs, qk]
            summed = (mine + jnp.transpose(theirs)).astype(BF16)
            right = buf2[l].reshape(4 * T, T)
            left = buf2[pk].reshape(4 * T, T)
            half = lax.dot_general(
                summed, right, (((1,), (1,)), ((), ())), preferred_element_type=F32
            ).astype(BF16)
            ladder = jnp.zeros((T, T), F32)
            for q in range(4):
                ladder += jnp.dot(
                    left[q * T : (q + 1) * T], half[:, q * T : (q + 1) * T], preferred_element_type=F32
                )
            ladder = ladder.astype(BF16).astype(F32)
            live = jnp.logical_and(pk < length, l < length)

            def update(side, block, ladder, den, old):
                target = drv[side, block] + ladder
                resid = jnp.where(live, target - den * old, 0.0)
                new = jnp.where(live, target / den, 0.0).astype(BF16).astype(F32)
                cur[side, block] = new
                return jnp.sum(resid * resid, keepdims=True)

            first = update(ps, pk, ladder, e_col[pk] + e_row[l] - occ, mine)
            second = update(qs, qk, jnp.transpose(ladder), e_col[l] + e_row[pk] - occ, theirs)
            return first, jnp.where(partner_counts, second, 0.0)

        for it in range(2):
            totals = [jnp.zeros((1, 1), F32), jnp.zeros((1, 1), F32)]
            for k in range(2):
                l = jnp.where(jnp.logical_or(diag, my_t == 0), k, 1 - k)
                qs = jnp.where(diag, 0, 1)
                first, second = block_step(it, 0, k, qs, l, l, jnp.logical_not(diag))
                totals = [totals[0] + first, totals[1] + second]
            for s in range(2):
                nacc[it, s] = jnp.broadcast_to(totals[s], (1, T))

            @pl.when(diag)
            def _():
                first, second = block_step(it, 1, 0, 1, 1, 1, True)
                nacc[it, 1] = jnp.broadcast_to(first + second, (1, T))

        sub = lax.broadcasted_iota(I32, (8, T), 0)
        for s in range(2):
            extra = jnp.zeros((8, T), F32)
            for it in range(2):
                total = jnp.broadcast_to(nacc[it, s], (8, T))
                high = total.astype(BF16).astype(F32)
                extra = jnp.where(sub == 2 * it, high, jnp.where(sub == 2 * it + 1, total - high, extra))
            rows = cur[s].reshape(NV, 8, T)
            message = jnp.concatenate([rows, jnp.broadcast_to(extra[None], (NV, 8, T))], axis=1)
            osend[s] = message.astype(BF16)

        def out_copy(s, w):
            row = my_i if s == 0 else jnp.where(diag, my_i, my_j)
            col = my_j if s == 0 else my_i
            half = lax.rem(lax.div(w, 16) + jnp.where(diag, s, my_t), 2)
            return row, orecv.at[col, half], jnp.logical_and(row == p, w == v)

        for s in range(2):
            @pl.loop(0, NV)
            def _(w):
                row, dst, self_home = out_copy(s, w)

                @pl.when(jnp.logical_not(self_home))
                def _():
                    remote(osend.at[s, w], dst, s_out, r_out, row, w).start()

                @pl.when(self_home)
                def _():
                    pltpu.make_async_copy(osend.at[s, w], dst, r_out).start()

    pltpu.make_async_copy(orecv, orecv, r_out).wait()
    totals = [jnp.zeros((1, T), F32), jnp.zeros((1, T), F32)]
    count = jnp.ones((1, T), F32)
    for s in range(NO):
        j = order[0, s]
        pieces = [orecv[j, h].astype(F32) for h in range(2)]
        out[0, s] = jnp.concatenate([piece[:8] for piece in pieces], axis=1).astype(BF16)
        both = pieces[0][8:] + pieces[1][8:]
        totals = [
            jnp.where(lane == s, both[2 * it : 2 * it + 1] + both[2 * it + 1 : 2 * it + 2], totals[it])
            for it in range(2)
        ]
        size = (lens[0, j] * T).astype(F32)
        count = jnp.where(lane == s, size * size, count)
    for it in range(2):
        norms[it] = jnp.sqrt(totals[it] / count + 1e-6)[:, :NO]

    for d, cj, h, pp, vv, side, own in targets:
        away(own, lambda: amp_copy(2 * d + cj, h, side, pp, vv).wait_send())
    for dz in range(1, NZ):
        tab_copy(dz).wait_send()

    @pl.when(jnp.logical_not(host))
    def _():
        tab_copy(0).wait_send()

    @pl.when(host)
    def _():
        @pl.loop(1, NV)
        def _(d):
            slice_copy(lax.rem(v + d, NV)).wait_send()

        @pl.loop(1, NV)
        def _(d):
            ev_copy(lax.rem(v + d, NV)).wait_send()

        for dz in range(1, NZ):
            remote(sel.at[dz], buf2.at[:, z], s_sel, r_sel, p, v).wait_send()
        for s in range(2):
            @pl.loop(0, NV)
            def _(w):
                row = my_i if s == 0 else jnp.where(diag, my_i, my_j)

                @pl.when(jnp.logical_not(jnp.logical_and(row == p, w == v)))
                def _():
                    remote(osend.at[s, w], osend.at[s, w], s_out, r_out, row, w).wait_send()


def shards(lam, drive, order, dom_tiles, dom_len, factors, e_occ, e_virt):
    vmem, smem = pl.BlockSpec(memory_space=pltpu.VMEM), pl.BlockSpec(memory_space=pltpu.SMEM)
    sem = pltpu.SemaphoreType.DMA
    return pl.pallas_call(
        kernel,
        out_shape=(
            jax.ShapeDtypeStruct((1, NO, 8, 2 * T), BF16),
            jax.ShapeDtypeStruct((2, 1, NO), F32),
        ),
        in_specs=[vmem, vmem, smem, smem, smem, pl.BlockSpec(memory_space=pl.ANY), smem, vmem],
        out_specs=(vmem, vmem),
        scratch_shapes=[
            pltpu.VMEM((NO, 2, 16, T), BF16),
            pltpu.VMEM((2, NV, 16, T), BF16),
            pltpu.VMEM((NV, 64, T), BF16),
            pltpu.VMEM((NZ, 2, 64, T), BF16),
            pltpu.VMEM((2, NZ, 64, T), BF16),
            pltpu.VMEM((1, T), F32),
            pltpu.VMEM((NV, 1, T), F32),
            pltpu.VMEM((1, T), I32),
            pltpu.VMEM((NO, 1, T), I32),
            pltpu.SMEM((NO, 1, T), I32),
            pltpu.VMEM((2, 2, T, T), F32),
            pltpu.VMEM((2, 2, T, T), F32),
            pltpu.VMEM((2, 1, T), F32),
            pltpu.VMEM((2, T, T), F32),
            pltpu.VMEM((2, 2, 1, T), F32),
            pltpu.VMEM((2, NV, 16, T), BF16),
            pltpu.VMEM((NO, 2, 16, T), BF16),
        ]
        + [sem] * 13,
        compiler_params=pltpu.CompilerParams(
            collective_id=0, has_side_effects=True, vmem_limit_bytes=24 << 20
        ),
    )(lam, drive, order, dom_tiles, dom_len, factors, e_occ, e_virt)


def solution(mesh):
    return jax.shard_map(
        shards,
        mesh=mesh,
        in_specs=(
            P("pair", None, "virt", None),
            P("pair", None, "virt", None),
            P("pair", None),
            P("pair", None, None),
            P("pair", None),
            P("virt", None, None, None),
            P(),
            P("virt", None),
        ),
        out_specs=(P("pair", None, "virt", None), P(None, "pair", None)),
        check_vma=False,
    )
```

time: 535 us -> 52.1 us (0.10)
  the two profiles are of different devices: /device:TPU:8 before, /device:TPU:1 now
where the time goes in v1:
time: 52.1 us; the launch traced here: 51.9 us
  Pallas kernels  46.6 us (89%)
  local copies, waits for them, and re-layouts  4.63 us (9%)
  between operations  0.69 us (1%)
    pallas_call x1, Pallas kernels, shards(): pl.pallas_call(kernel, out_shape=(jax.ShapeDtypeStruct((1, NO, 8, 2 * T),...  46.6 us
    unnamed x17, local copies, waits for them, and re-layouts  4.63 us

profile of v1, /device:TPU:1, one launch (start us, length us, event | category | flops | bytes accessed | tf_op | source)
XLA Modules:
  0.0 51.9 jit_solution(4996077894854274932)
XLA Ops:
  0.6 0.0 copy-start.6
  0.6 0.0 copy-start.5
  0.7 0.0 copy-start.4
  0.7 0.0 copy-start.3
  0.7 0.8 %copy.10.tiles = s32[1,16,2]{2,1,0:T(8,128)S(1)} copy(s32[1,16,2]{1,2,0:T(2,128)} %param.11) | data formatting | bytes 256 | tf_op args[3]
  1.5 0.0 copy-done.6
  1.5 0.0 copy-done.5
  1.5 0.0 copy-done.4
  1.5 0.0 copy-done.3
  1.5 0.0 copy-start
  1.5 0.9 %copy-done = f32[1,16,8,256]{3,2,1,0:T(8,128)S(1)} copy-done((f32[1,16,8,256]{3,2,1,0:T(8,128)S(1)}, f32[1,16,8,256]{3,2,1,0:T(8,128)}, u32[]{:S(2)}) %copy-start) | copy-done | bytes 131096
  2.4 0.0 copy-start.1
  2.4 0.9 %copy-done.1 = bf16[1,4,128,128]{3,2,1,0:T(8,128)(2,1)S(1)} copy-done((bf16[1,4,128,128]{3,2,1,0:T(8,128)(2,1)S(1)}, bf16[1,4,128,128]{3,2,1,0:T(8,128)(2,1)}, u32[]{:S(2)}) %copy-start.1) | copy-done | bytes 131096
  3.3 0.0 copy-start.2
  3.3 0.8 %copy-done.2 = bf16[1,16,8,256]{3,2,1,0:T(8,128)(2,1)S(1)} copy-done((bf16[1,16,8,256]{3,2,1,0:T(8,128)(2,1)S(1)}, bf16[1,16,8,256]{3,2,1,0:T(8,128)(2,1)}, u32[]{:S(2)}) %copy-start.2) | copy-done | bytes 65560
  4.1 46.6 %shard_map.95 = (bf16[1,16,8,256]{3,2,1,0:T(8,128)(2,1)S(1)}, f32[2,1,16]{2,1,0:T(1,128)S(1)}) custom-call(bf16[1,16,8,256]{3,2,1,0:T(8,128)(2,1)S(1)} %copy-done.2, f32[1,16,8,256]{3,2,1,0:T(8,128)S(1)} %copy-done, s32[1,16]{1,0:T(1,128)S(1)} %copy-done.3, s32[1,16,2]{2,1,0:T(8,128)S(1)} %copy.10.tiles, s32[1,16]{1,0:T(1,128)S(1)} %copy-done.4, ...), custom_call_target="tpu_custom_call" | custom-call | tf_op jit(solution)/shard_map/pallas_call | solution.py:349
  50.7 0.6 %copy.13 = bf16[1,16,8,256]{3,2,1,0:T(8,128)(2,1)} copy(bf16[1,16,8,256]{3,2,1,0:T(8,128)(2,1)S(1)} %get-tuple-element.4) | data formatting | bytes 131072
  51.3 0.6 %copy.14 = f32[2,1,16]{2,1,0:T(1,128)} copy(f32[2,1,16]{2,1,0:T(1,128)S(1)} %get-tuple-element.5) | data formatting | bytes 256
Async XLA Ops:
  0.6 0.8 %copy-start.6 = (bf16[1,128]{1,0:T(2,128)(2,1)S(1)}, bf16[1,128]{1,0:T(2,128)(2,1)}, u32[]{:S(2)}) copy-start(bf16[1,128]{1,0:T(2,128)(2,1)} %e_virt.1) | copy-start | bytes 772
  0.6 0.8 %copy-start.5 = (f32[16]{0:T(128)S(1)}, f32[16]{0:T(128)}, u32[]{:S(2)}) copy-start(f32[16]{0:T(128)} %e_occ.1) | copy-start | bytes 196
  0.7 0.8 %copy-start.4 = (s32[1,16]{1,0:T(1,128)S(1)}, s32[1,16]{1,0:T(1,128)}, u32[]{:S(2)}) copy-start(s32[1,16]{1,0:T(1,128)} %lens.1) | copy-start | bytes 196
  0.7 0.8 %copy-start.3 = (s32[1,16]{1,0:T(1,128)S(1)}, s32[1,16]{1,0:T(1,128)}, u32[]{:S(2)}) copy-start(s32[1,16]{1,0:T(1,128)} %order.1) | copy-start | bytes 196
  1.5 0.9 %copy-start = (f32[1,16,8,256]{3,2,1,0:T(8,128)S(1)}, f32[1,16,8,256]{3,2,1,0:T(8,128)}, u32[]{:S(2)}) copy-start(f32[1,16,8,256]{3,2,1,0:T(8,128)} %drive.1) | copy-start | bytes 393220
  2.4 0.9 %copy-start.1 = (bf16[1,4,128,128]{3,2,1,0:T(8,128)(2,1)S(1)}, bf16[1,4,128,128]{3,2,1,0:T(8,128)(2,1)}, u32[]{:S(2)}) copy-start(bf16[1,4,128,128]{3,2,1,0:T(8,128)(2,1)} %factors.1) | copy-start | bytes 393220
  3.3 0.8 %copy-start.2 = (bf16[1,16,8,256]{3,2,1,0:T(8,128)(2,1)S(1)}, bf16[1,16,8,256]{3,2,1,0:T(8,128)(2,1)}, u32[]{:S(2)}) copy-start(bf16[1,16,8,256]{3,2,1,0:T(8,128)(2,1)} %lam.1) | copy-start | bytes 196612

commit v2 on v1

v2 whole, which is shorter than its diff:
```python
import functools

import jax
import jax.numpy as jnp
from jax import lax
from jax.experimental import pallas as pl
from jax.experimental.pallas import tpu as pltpu
from jax.sharding import PartitionSpec as P

F32, BF16, I32 = jnp.float32, jnp.bfloat16, jnp.int32
MESH = pl.DeviceIdType.MESH
NZ, NV, NO, T = 8, 32, 16, 128
Y_ORDER = (4, 3, 5, 2, 6, 1, 7)
Y_NEAR = (1, 7, 2, 6, 3, 5, 4)


def host_of(z, c, d, cj, ty):
    if d == 0:
        diag = c == cj
        g = jnp.where(diag, 1, 0)
        t = jnp.where(diag, c, ty)
        return z, 2 * g + t, jnp.where(diag, ty, c)
    if d < 4:
        zh = lax.rem(z + (d >= 2), NZ) if d >= 2 else z
        return zh, 2 * (2 + 4 * (d - 1) + 2 * c + cj) + ty, 0
    if d > 4:
        e = NZ - d
        zh = lax.rem(z + d + (e >= 2), NZ)
        return zh, 2 * (2 + 4 * (e - 1) + 2 * cj + c) + ty, 1
    low = z < 4
    c_low, c_high = jnp.where(low, c, cj), jnp.where(low, cj, c)
    zh = lax.rem(lax.rem(z, 4) + 2 + 4 * c_low, NZ)
    return zh, 2 * (14 + c_high) + ty, jnp.where(low, 0, 1)


def pair_of(zh, v):
    g, t = lax.div(v, 2), lax.rem(v, 2)
    b = jnp.maximum(g - 2, 0)
    d = lax.div(b, 4) + 1
    z_mid = lax.rem(zh + NZ - jnp.where(d >= 2, 1, 0), NZ)
    i_mid = 2 * z_mid + lax.rem(lax.div(b, 2), 2)
    j_mid = 2 * lax.rem(z_mid + d, NZ) + lax.rem(b, 2)
    zl = lax.rem(zh + 6, NZ)
    z_far = lax.rem(zl, 4)
    i_far = 2 * z_far + lax.div(zl, 4)
    j_far = 2 * (z_far + 4) + (g - 14)
    i = jnp.where(g == 0, 2 * zh, jnp.where(g == 1, 2 * zh + t, jnp.where(g >= 14, i_far, i_mid)))
    j = jnp.where(g == 0, 2 * zh + 1, jnp.where(g == 1, 2 * zh + t, jnp.where(g >= 14, j_far, j_mid)))
    return i, j


def kernel(
    lam_in, drive_in, order_in, tiles_in, lens_in, factors, e_occ_in, e_virt_in,
    out, norms,
    lam, drive, order, tiles, lens, e_occ, e_virt,
    send, recv, buf1, sel, buf2, ev_own, evb, tab_own, tab, tab_s, cur, drv, den, inv, osend, orecv,
    s_amp, r_amp, s_fac, r_fac, r_line, s_ev, r_ev, s_tab, r_tab, s_sel, r_sel, s_out, r_out, l_sem, in_sems, go,
):
    p, v = lax.axis_index("pair"), lax.axis_index("virt")
    z, c = lax.div(p, 2), lax.rem(p, 2)
    x, y = lax.div(v, 8), lax.rem(v, 8)
    k_own = lax.div(v, 16)
    host = c == 1
    my_i, my_j = pair_of(z, v)
    my_t = lax.rem(v, 2)
    diag = lax.div(v, 2) == 1
    row_1 = jnp.where(diag, my_i, my_j)

    def remote(src, dst, ss, rs, pp, vv):
        return pltpu.make_async_remote_copy(
            src_ref=src, dst_ref=dst, send_sem=ss, recv_sem=rs,
            device_id={"pair": pp, "virt": vv}, device_id_type=MESH,
        )

    def drain(ref, sem):
        pltpu.make_async_copy(ref, ref, sem).wait()

    loads = [
        pltpu.make_async_copy(src, dst, in_sems.at[n])
        for n, (src, dst) in enumerate([
            (tiles_in, tiles), (lens_in, lens), (order_in, order), (lam_in, lam), (drive_in, drive),
            (e_virt_in, e_virt), (e_occ_in, e_occ),
        ])
    ]
    for load in loads:
        load.start()

    barrier = pltpu.get_barrier_semaphore()

    def greet(pp, vv):
        pl.semaphore_signal(barrier, inc=1, device_id={"pair": pp, "virt": vv}, device_id_type=MESH)

    def at_y(dy):
        return 8 * x + lax.rem(y + dy, 8)

    def at_x(dx):
        return 8 * lax.rem(x + dx, 4) + y

    def at_z(dz):
        return 2 * lax.rem(z + dz, NZ) + 1

    @pl.when(host)
    def _():
        for dy in Y_ORDER:
            greet(p, at_y(dy))
        for dx in (2, 1, 3):
            greet(p, at_x(dx))
        for dz in Y_ORDER:
            greet(at_z(dz), v)

        @pl.loop(0, NZ)
        def _(zz):
            greet(2 * zz, v)

        @pl.loop(0, NV)
        def _(w):
            greet(2 * lax.div(my_i, 2), w)
            greet(2 * lax.div(row_1, 2), w)

    targets = []
    for d in range(NZ):
        for cj in range(2):
            for h in range(2):
                zh, vh, side = host_of(z, c, d, cj, lax.rem(k_own + h, 2))
                own = jnp.logical_and(host, vh == v) if d < 2 else None
                targets.append((2 * d + cj, h, 2 * zh + 1, vh, side, own))

    def away(own, act):
        if own is None:
            act()
        else:
            pl.when(jnp.logical_not(own))(act)

    for load in loads[:2]:
        load.wait()
    lane = lax.broadcasted_iota(I32, (1, T), 1)
    row_table = jnp.zeros((1, T), I32)
    for j in range(NO):
        for k in range(2):
            row_table = jnp.where(lane == 2 * j + k, tiles[0, k, j], row_table)
        row_table = jnp.where(lane == 32 + j, lens[0, j], row_table)
    tab_own[...] = row_table

    my_slice = factors.at[0, lax.div(z, 2), pl.ds(pl.multiple_of(64 * lax.rem(z, 2), 64), 64)]

    def tab_copy(dz):
        return remote(tab_own, tab.at[p], s_tab, r_tab, at_z(dz), v)

    @pl.when(host)
    def _():
        pl.semaphore_wait(barrier, 7 + 3 + 7)
        for dy in Y_ORDER:
            remote(my_slice, buf1.at[v], s_fac, r_line.at[dy], p, at_y(dy)).start()
        for dx in (2, 1, 3):
            remote(my_slice, buf1.at[v], s_fac, r_fac, p, at_x(dx)).start()
        pltpu.make_async_copy(my_slice, buf1.at[v], r_fac).start()
        pltpu.make_async_copy(tab_own, tab.at[p], r_tab).start()
        for dz in Y_ORDER:
            tab_copy(dz).start()

    for load in loads[2:]:
        load.wait()
    ev_own[...] = e_virt[...].astype(F32)

    def find(s, found):
        o = order[0, s]
        return tuple(
            jnp.where(o == 2 * lax.rem(z + n // 2, NZ) + n % 2, s, f) for n, f in enumerate(found)
        )

    slots = lax.fori_loop(0, NO, find, (jnp.int32(0),) * NO)
    for n in range(NO):
        own_lam = lam[0, slots[n]].astype(F32)
        own_drive = drive[0, slots[n]]
        for h in range(2):
            cols = slice(h * T, (h + 1) * T)
            send[n, h] = jnp.concatenate([own_lam[:, cols], own_drive[:, cols]], axis=0).astype(BF16)

    @pl.when(host)
    def _():
        for dy in Y_NEAR:
            source = at_y(8 - dy)
            drain(buf1.at[source], r_line.at[dy])
            for dx in (2, 1, 3):
                remote(buf1.at[source], buf1.at[source], s_fac, r_fac, p, at_x(dx)).start()
        pl.semaphore_wait(go, 1)

    @pl.when(jnp.logical_not(host))
    def _():
        pl.semaphore_wait(barrier, NZ + 2 * NV)
        pl.semaphore_signal(go, inc=1, device_id={"pair": p + 1, "virt": v}, device_id_type=MESH)
        tab_copy(0).start()
        for dz in Y_ORDER:
            tab_copy(dz).start()

    def amp_copy(n, h, side, pp, vv):
        return remote(send.at[n, h], recv.at[side, v], s_amp, r_amp, pp, vv)

    def ev_copy(pp, vv):
        return remote(ev_own, evb.at[v], s_ev, r_ev, pp, vv)

    def when_first(side, act):
        if isinstance(side, int):
            if side == 0:
                act()
        else:
            pl.when(side == 0)(act)

    for n, h, pp, vv, side, own in targets:
        def send_away():
            amp_copy(n, h, side, pp, vv).start()
            when_first(side, lambda: ev_copy(pp, vv).start())

        away(own, send_away)
        if own is not None:
            @pl.when(own)
            def _():
                pltpu.make_async_copy(send.at[n, h], recv.at[side, v], r_amp).start()
                when_first(side, lambda: pltpu.make_async_copy(ev_own, evb.at[v], r_ev).start())

    @pl.when(host)
    def _():
        drain(tab, r_tab)
        to_smem = pltpu.make_async_copy(tab, tab_s, l_sem)
        to_smem.start()
        to_smem.wait()
        drain(buf1.at[0 : 1 + 3 * 8], r_fac)
        for dz in Y_ORDER:
            zd = lax.rem(z + dz, NZ)
            i, j = pair_of(zd, v)
            for k in range(2):
                sel[dz, k] = buf1[tab_s[i, 0, 2 * j + k]]
            remote(sel.at[dz], buf2.at[:, z], s_sel, r_sel, 2 * zd + 1, v).start()
        own_tiles = [tab_s[my_i, 0, 2 * my_j + k] for k in range(2)]
        for k in range(2):
            sel[0, k] = buf1[own_tiles[k]]
        pltpu.make_async_copy(sel.at[0], buf2.at[:, z], r_sel).start()
        length = tab_s[my_i, 0, 32 + my_j]
        occ = e_occ[my_i] + e_occ[my_j]
        drain(evb, r_ev)
        e_row = [evb[tile] for tile in own_tiles]
        e_col = [jnp.transpose(jnp.broadcast_to(e, (T, T))) for e in e_row]
        drain(recv, r_amp)

        crossed = jnp.logical_and(jnp.logical_not(diag), my_t == 1)
        couples = [
            (0, 0, jnp.where(diag, 0, 1), jnp.where(crossed, 1, 0)),
            (0, 1, jnp.where(diag, 0, 1), jnp.where(crossed, 0, 1)),
            (1, 0, 1, 1),
        ]

        def alive(pk, l):
            return jnp.logical_and(pk < length, l < length)

        def prepare(o):
            ps, pk, qs, l = couples[o]
            first = recv[ps, pl.ds(16 * pk, 16)].astype(F32).reshape(16, 2, 8, T)
            second = recv[qs, pl.ds(16 * l, 16)].astype(F32).reshape(16, 2, 8, T)
            live = alive(pk, l)
            cur[o, 0] = jnp.where(live, first[:, 0].reshape(T, T), 0.0)
            cur[o, 1] = jnp.where(live, jnp.transpose(second[:, 0].reshape(T, T)), 0.0)
            drv[o, 0] = first[:, 1].reshape(T, T)
            drv[o, 1] = jnp.transpose(second[:, 1].reshape(T, T))
            e_l = jnp.where(l == 0, e_row[0], e_row[1])
            den[o] = e_col[pk] + e_l - occ
            inv[o] = 1.0 / den[o]

        def iterate(o):
            ps, pk, qs, l = couples[o]
            right = buf2[l].reshape(4 * T, T)
            left = buf2[pk].reshape(4 * T, T)
            live = alive(pk, l)
            now = [cur[o, 0], cur[o, 1]]
            squares = []
            for it in range(2):
                half = lax.dot_general(
                    (now[0] + now[1]).astype(BF16), right, (((1,), (1,)), ((), ())),
                    preferred_element_type=F32,
                ).astype(BF16)
                ladder = jnp.zeros((T, T), F32)
                for q in range(4):
                    rows = slice(q * T, (q + 1) * T)
                    ladder += jnp.dot(left[rows], half[:, rows], preferred_element_type=F32)
                ladder = ladder.astype(BF16).astype(F32)
                for n in range(2):
                    target = drv[o, n] + ladder
                    resid = jnp.where(live, target - den[o] * now[n], 0.0)
                    now[n] = jnp.where(live, target * inv[o], 0.0).astype(BF16).astype(F32)
                    squares.append(jnp.sum(resid * resid, keepdims=True))
            return now[0], jnp.transpose(now[1]), squares

        def norm_rows(first, second):
            rows = jnp.zeros((8, T), F32)
            sub = lax.broadcasted_iota(I32, (8, T), 0)
            for it, total in enumerate((first, second)):
                total = jnp.broadcast_to(total, (8, T))
                high = total.astype(BF16).astype(F32)
                rows = jnp.where(sub == 2 * it, high, jnp.where(sub == 2 * it + 1, total - high, rows))
            return jnp.broadcast_to(rows[None], (16, 8, T))

        def post(side, block, values, rows):
            message = jnp.concatenate([values.reshape(16, 8, T), rows], axis=1)
            osend[side, pl.ds(16 * block, 16)] = message.astype(BF16)

        for o in range(2):
            prepare(o)
        pl.when(diag)(lambda: prepare(2))
        drain(buf2, r_sel)
        done = [iterate(o) for o in range(2)]
        sums = [done[0][2][n] + done[1][2][n] for n in range(4)]
        rows = norm_rows(sums[0], sums[2])
        for o in range(2):
            post(0, o, done[o][0], rows)

        @pl.when(jnp.logical_not(diag))
        def _():
            rows = norm_rows(sums[1], sums[3])
            for o in range(2):
                post(1, couples[o][3], done[o][1], rows)

        @pl.when(diag)
        def _():
            first, second, squares = iterate(2)
            rows = norm_rows(squares[0] + squares[1], squares[2] + squares[3])
            post(1, 0, first, rows)
            post(1, 1, second, rows)

        for s in range(2):
            row, col = (my_i, my_j) if s == 0 else (row_1, my_i)

            @pl.loop(0, NV)
            def _(w):
                half = lax.rem(lax.div(w, 16) + jnp.where(diag, s, my_t), 2)
                dst = orecv.at[col, half]
                self_home = jnp.logical_and(row == p, w == v)

                @pl.when(jnp.logical_not(self_home))
                def _():
                    remote(osend.at[s, w], dst, s_out, r_out, row, w).start()

                @pl.when(self_home)
                def _():
                    pltpu.make_async_copy(osend.at[s, w], dst, r_out).start()

    for n, h, pp, vv, side, own in targets:
        def left():
            amp_copy(n, h, side, pp, vv).wait_send()
            when_first(side, lambda: ev_copy(pp, vv).wait_send())

        away(own, left)
    for dz in range(1, NZ):
        tab_copy(dz).wait_send()

    @pl.when(jnp.logical_not(host))
    def _():
        tab_copy(0).wait_send()

    @pl.when(host)
    def _():
        drain(buf1.at[0 : 7 + 3 * 8], s_fac)
        drain(sel.at[0 : NZ - 1], s_sel)
        for s in range(2):
            row = my_i if s == 0 else row_1

            @pl.loop(0, NV)
            def _(w):
                @pl.when(jnp.logical_not(jnp.logical_and(row == p, w == v)))
                def _():
                    remote(osend.at[s, w], osend.at[s, w], s_out, r_out, row, w).wait_send()

    drain(orecv, r_out)
    totals = [jnp.zeros((1, T), F32), jnp.zeros((1, T), F32)]
    count = jnp.ones((1, T), F32)
    for s in range(NO):
        j = order[0, s]
        pieces = [orecv[j, h].astype(F32) for h in range(2)]
        out[0, s] = jnp.concatenate([piece[:8] for piece in pieces], axis=1).astype(BF16)
        both = pieces[0][8:] + pieces[1][8:]
        totals = [
            jnp.where(lane == s, both[2 * it : 2 * it + 1] + both[2 * it + 1 : 2 * it + 2], totals[it])
            for it in range(2)
        ]
        size = (lens[0, j] * T).astype(F32)
        count = jnp.where(lane == s, size * size, count)
    for it in range(2):
        norms[it] = jnp.sqrt(totals[it] / count + 1e-6)[:, :NO]


def shards(lam, drive, order, dom_tiles, dom_len, factors, e_occ, e_virt):
    vmem = pl.BlockSpec(memory_space=pltpu.VMEM)
    sem = pltpu.SemaphoreType.DMA
    return pl.pallas_call(
        kernel,
        out_shape=(
            jax.ShapeDtypeStruct((1, NO, 8, 2 * T), BF16),
            jax.ShapeDtypeStruct((2, 1, NO), F32),
        ),
        in_specs=[pl.BlockSpec(memory_space=pltpu.HBM)] * 8,
        out_specs=(vmem, vmem),
        scratch_shapes=[
            pltpu.VMEM((1, NO, 8, 2 * T), BF16),
            pltpu.VMEM((1, NO, 8, 2 * T), F32),
            pltpu.SMEM((1, NO), I32),
            pltpu.SMEM((1, 2, NO), I32),
            pltpu.SMEM((1, NO), I32),
            pltpu.SMEM((NO,), F32),
            pltpu.VMEM((1, T), BF16),
            pltpu.VMEM((NO, 2, 16, T), BF16),
            pltpu.VMEM((2, NV, 16, T), BF16),
            pltpu.VMEM((NV, 64, T), BF16),
            pltpu.VMEM((NZ, 2, 64, T), BF16),
            pltpu.VMEM((2, NZ, 64, T), BF16),
            pltpu.VMEM((1, T), F32),
            pltpu.VMEM((NV, 1, T), F32),
            pltpu.VMEM((1, T), I32),
            pltpu.VMEM((NO, 1, T), I32),
            pltpu.SMEM((NO, 1, T), I32),
            pltpu.VMEM((3, 2, T, T), F32),
            pltpu.VMEM((3, 2, T, T), F32),
            pltpu.VMEM((3, T, T), F32),
            pltpu.VMEM((3, T, T), F32),
            pltpu.VMEM((2, NV, 16, T), BF16),
            pltpu.VMEM((NO, 2, 16, T), BF16),
        ]
        + [sem] * 4
        + [sem((8,))]
        + [sem] * 9
        + [sem((7,)), pltpu.SemaphoreType.REGULAR],
        compiler_params=pltpu.CompilerParams(
            collective_id=0, has_side_effects=True, vmem_limit_bytes=64 << 20
        ),
    )(lam, drive, order, jnp.swapaxes(dom_tiles, 1, 2), dom_len, factors, e_occ, e_virt)


def solution(mesh):
    return jax.shard_map(
        shards,
        mesh=mesh,
        in_specs=(
            P("pair", None, "virt", None),
            P("pair", None, "virt", None),
            P("pair", None),
            P("pair", None, None),
            P("pair", None),
            P("virt", None, None, None),
            P(),
            P("virt", None),
        ),
        out_specs=(P("pair", None, "virt", None), P(None, "pair", None)),
        check_vma=False,
    )
```

time: 52.1 us -> 41.7 us (0.80)
  Pallas kernels: 46.6 us -> 38.8 us
  local copies, waits for them, and re-layouts: 4.63 us -> 2.04 us
    pallas_call x1, Pallas kernels: 46.6 us -> 38.8 us  [shards(): pl.pallas_call(kernel, out_shape=(jax.ShapeDtypeStruct((1, NO, 8, 2 * T),...]
    unnamed x17 -> x4, local copies, waits for them, and re-layouts: 4.63 us -> 2.04 us
where the time goes in v2:
time: 41.7 us; the launch traced here: 41.5 us
  Pallas kernels  38.8 us (93%)
  local copies, waits for them, and re-layouts  2.04 us (5%)
  between operations  0.65 us (2%)
    pallas_call x1, Pallas kernels, shards(): pl.pallas_call(kernel, out_shape=(jax.ShapeDtypeStruct((1, NO, 8, 2 * T),...  38.8 us
    unnamed x4, local copies, waits for them, and re-layouts  2.04 us

profile of v2, /device:TPU:1, one launch (start us, length us, event | category | flops | bytes accessed | tf_op | source)
XLA Modules:
  0.0 41.5 jit_solution(5901327217154730307)
XLA Ops:
  0.6 38.8 %shard_map.95 = (bf16[1,16,8,256]{3,2,1,0:T(8,128)(2,1)}, f32[2,1,16]{2,1,0:T(1,128)}) custom-call(bf16[1,16,8,256]{3,2,1,0:T(8,128)(2,1)} %lam_in.1, f32[1,16,8,256]{3,2,1,0:T(8,128)} %drive_in.1, s32[1,16]{1,0:T(1,128)} %order_in.1, s32[1,2,16]{2,1,0:T(2,128)} %bitcast.1, s32[1,16]{1,0:T(1,128)} %lens_in.1, bf16[1,4,128,128]{3,2,1,0:T(8,128)(2,1)} %factors.1, ...), custom_call_target="tpu_custom_call" | custom-call | tf_op jit(solution)/shard_map/pallas_call | solution.py:392
  39.5 0.0 copy-start
  39.5 1.5 %copy.12 = bf16[1,16,8,256]{3,2,1,0:T(8,128)(2,1)} copy(bf16[1,16,8,256]{3,2,1,0:T(8,128)(2,1)} %get-tuple-element.4) | data formatting | bytes 131072
  40.9 0.0 copy-done
  41.0 0.6 %copy.13 = f32[2,1,16]{2,1,0:T(1,128)} copy(f32[2,1,16]{2,1,0:T(1,128)S(1)} %copy-done) | data formatting | bytes 256
Async XLA Ops:
  39.5 1.5 %copy-start = (f32[2,1,16]{2,1,0:T(1,128)S(1)}, f32[2,1,16]{2,1,0:T(1,128)}, u32[]{:S(2)}) copy-start(f32[2,1,16]{2,1,0:T(1,128)} %get-tuple-element.5) | copy-start | bytes 388

commit v3 on v2

--- a/solution.py
+++ b/solution.py
@@ -11,7 +11,7 @@
 MESH = pl.DeviceIdType.MESH
 NZ, NV, NO, T = 8, 32, 16, 128
 Y_ORDER = (4, 3, 5, 2, 6, 1, 7)
-Y_NEAR = (1, 7, 2, 6, 3, 5, 4)
+X_ORDER = (2, 1, 3)
 
 
 def host_of(z, c, d, cj, ty):
@@ -53,8 +53,8 @@
     lam_in, drive_in, order_in, tiles_in, lens_in, factors, e_occ_in, e_virt_in,
     out, norms,
     lam, drive, order, tiles, lens, e_occ, e_virt,
-    send, recv, buf1, sel, buf2, ev_own, evb, tab_own, tab, tab_s, cur, drv, den, inv, osend, orecv,
-    s_amp, r_amp, s_fac, r_fac, r_line, s_ev, r_ev, s_tab, r_tab, s_sel, r_sel, s_out, r_out, l_sem, in_sems, go,
+    send, recv, buf1, sel, buf2, ev_own, evb, tab_own, tab, tab_s, ids, cur, drv, den, inv, osend, orecv,
+    s_amp, r_amp, s_fac, r_fac, s_ev, r_ev, s_tab, r_tab, s_sel, r_sel, s_out, r_out, l_sem, in_sems, go,
 ):
     p, v = lax.axis_index("pair"), lax.axis_index("virt")
     z, c = lax.div(p, 2), lax.rem(p, 2)
@@ -90,32 +90,25 @@
     def greet(pp, vv):
         pl.semaphore_signal(barrier, inc=1, device_id={"pair": pp, "virt": vv}, device_id_type=MESH)
 
-    def at_y(dy):
-        return 8 * x + lax.rem(y + dy, 8)
-
-    def at_x(dx):
-        return 8 * lax.rem(x + dx, 4) + y
-
     def at_z(dz):
         return 2 * lax.rem(z + dz, NZ) + 1
 
+    def far_first(step):
+        a, b = lax.div(step, 4), lax.rem(step, 4)
+        dy = jnp.where(lax.rem(a, 2) == 1, 4 - lax.div(a + 1, 2), 4 + lax.div(a, 2))
+        dx = jnp.where(lax.rem(b, 2) == 1, 2 - lax.div(b + 1, 2), 2 + lax.div(b, 2))
+        return 8 * lax.rem(x + dx, 4) + lax.rem(y + dy, 8)
+
     @pl.when(host)
     def _():
-        for dy in Y_ORDER:
-            greet(p, at_y(dy))
-        for dx in (2, 1, 3):
-            greet(p, at_x(dx))
+        @pl.loop(0, NV - 1)
+        def _(step):
+            greet(p, far_first(step))
+
         for dz in Y_ORDER:
             greet(at_z(dz), v)
-
-        @pl.loop(0, NZ)
-        def _(zz):
-            greet(2 * zz, v)
-
-        @pl.loop(0, NV)
-        def _(w):
-            greet(2 * lax.div(my_i, 2), w)
-            greet(2 * lax.div(row_1, 2), w)
+            greet(at_z(dz) - 1, v)
+        greet(p - 1, v)
 
     targets = []
     for d in range(NZ):
@@ -141,22 +134,37 @@
         row_table = jnp.where(lane == 32 + j, lens[0, j], row_table)
     tab_own[...] = row_table
 
-    my_slice = factors.at[0, lax.div(z, 2), pl.ds(pl.multiple_of(64 * lax.rem(z, 2), 64), 64)]
+    my_rows = 4 * z + x
+
+    def slice_at(place):
+        rows = 4 * z + lax.div(place, 8)
+        return factors.at[0, pl.ds(pl.multiple_of(16 * rows, 16), 16)]
+
+    def slice_copy(place):
+        return remote(slice_at(place), buf1.at[v], s_fac, r_fac, p, place)
 
     def tab_copy(dz):
         return remote(tab_own, tab.at[p], s_tab, r_tab, at_z(dz), v)
 
     @pl.when(host)
     def _():
-        pl.semaphore_wait(barrier, 7 + 3 + 7)
-        for dy in Y_ORDER:
-            remote(my_slice, buf1.at[v], s_fac, r_line.at[dy], p, at_y(dy)).start()
-        for dx in (2, 1, 3):
-            remote(my_slice, buf1.at[v], s_fac, r_fac, p, at_x(dx)).start()
-        pltpu.make_async_copy(my_slice, buf1.at[v], r_fac).start()
-        pltpu.make_async_copy(tab_own, tab.at[p], r_tab).start()
+        pl.semaphore_wait(barrier, NV - 1 + NZ - 1)
         for dz in Y_ORDER:
             tab_copy(dz).start()
+
+        @pl.loop(0, NV - 1)
+        def _(step):
+            slice_copy(far_first(step)).start()
+
+        pltpu.make_async_copy(slice_at(v), buf1.at[v], r_fac).start()
+        pltpu.make_async_copy(tab_own, tab.at[p], r_tab).start()
+
+    @pl.when(jnp.logical_not(host))
+    def _():
+        pl.semaphore_wait(barrier, NZ)
+        for dz in Y_ORDER:
+            tab_copy(dz).start()
+        tab_copy(0).start()
 
     for load in loads[2:]:
         load.wait()
@@ -178,20 +186,12 @@
 
     @pl.when(host)
     def _():
-        for dy in Y_NEAR:
-            source = at_y(8 - dy)
-            drain(buf1.at[source], r_line.at[dy])
-            for dx in (2, 1, 3):
-                remote(buf1.at[source], buf1.at[source], s_fac, r_fac, p, at_x(dx)).start()
+        drain(tab, r_tab)
+        pl.semaphore_signal(go, inc=1, device_id={"pair": p - 1, "virt": v}, device_id_type=MESH)
+
+    @pl.when(jnp.logical_not(host))
+    def _():
         pl.semaphore_wait(go, 1)
-
-    @pl.when(jnp.logical_not(host))
-    def _():
-        pl.semaphore_wait(barrier, NZ + 2 * NV)
-        pl.semaphore_signal(go, inc=1, device_id={"pair": p + 1, "virt": v}, device_id_type=MESH)
-        tab_copy(0).start()
-        for dz in Y_ORDER:
-            tab_copy(dz).start()
 
     def amp_copy(n, h, side, pp, vv):
         return remote(send.at[n, h], recv.at[side, v], s_amp, r_amp, pp, vv)
@@ -220,21 +220,25 @@
 
     @pl.when(host)
     def _():
-        drain(tab, r_tab)
         to_smem = pltpu.make_async_copy(tab, tab_s, l_sem)
         to_smem.start()
         to_smem.wait()
-        drain(buf1.at[0 : 1 + 3 * 8], r_fac)
-        for dz in Y_ORDER:
-            zd = lax.rem(z + dz, NZ)
-            i, j = pair_of(zd, v)
+        places = [
+            (lax.rem(z + dz, NZ), 8 * lax.rem(x + dx, 4) + y) for dz in Y_ORDER + (0,) for dx in X_ORDER + (0,)
+        ]
+        for n, (zd, vd) in enumerate(places):
+            i, j = pair_of(zd, vd)
             for k in range(2):
-                sel[dz, k] = buf1[tab_s[i, 0, 2 * j + k]]
-            remote(sel.at[dz], buf2.at[:, z], s_sel, r_sel, 2 * zd + 1, v).start()
-        own_tiles = [tab_s[my_i, 0, 2 * my_j + k] for k in range(2)]
-        for k in range(2):
-            sel[0, k] = buf1[own_tiles[k]]
-        pltpu.make_async_copy(sel.at[0], buf2.at[:, z], r_sel).start()
+                ids[2 * n + k] = tab_s[i, 0, 2 * j + k]
+        own_tiles = [ids[62 + k] for k in range(2)]
+        drain(buf1, r_fac)
+        for n, (zd, vd) in enumerate(places):
+            for k in range(2):
+                sel[n, k] = buf1[ids[2 * n + k]]
+            if n < 31:
+                remote(sel.at[n], buf2.at[:, my_rows], s_sel, r_sel, 2 * zd + 1, vd).start()
+            else:
+                pltpu.make_async_copy(sel.at[n], buf2.at[:, my_rows], r_sel).start()
         length = tab_s[my_i, 0, 32 + my_j]
         occ = e_occ[my_i] + e_occ[my_j]
         drain(evb, r_ev)
@@ -357,8 +361,8 @@
 
     @pl.when(host)
     def _():
-        drain(buf1.at[0 : 7 + 3 * 8], s_fac)
-        drain(sel.at[0 : NZ - 1], s_sel)
+        drain(buf1.at[0 : NV - 1], s_fac)
+        drain(sel.at[0 : NV - 1], s_sel)
         for s in range(2):
             row = my_i if s == 0 else row_1
 
@@ -407,14 +411,15 @@
             pltpu.VMEM((1, T), BF16),
             pltpu.VMEM((NO, 2, 16, T), BF16),
             pltpu.VMEM((2, NV, 16, T), BF16),
-            pltpu.VMEM((NV, 64, T), BF16),
-            pltpu.VMEM((NZ, 2, 64, T), BF16),
-            pltpu.VMEM((2, NZ, 64, T), BF16),
+            pltpu.VMEM((NV, 16, T), BF16),
+            pltpu.VMEM((NV, 2, 16, T), BF16),
+            pltpu.VMEM((2, NV, 16, T), BF16),
             pltpu.VMEM((1, T), F32),
             pltpu.VMEM((NV, 1, T), F32),
             pltpu.VMEM((1, T), I32),
             pltpu.VMEM((NO, 1, T), I32),
             pltpu.SMEM((NO, 1, T), I32),
+            pltpu.SMEM((2 * NV,), I32),
             pltpu.VMEM((3, 2, T, T), F32),
             pltpu.VMEM((3, 2, T, T), F32),
             pltpu.VMEM((3, T, T), F32),
@@ -422,14 +427,12 @@
             pltpu.VMEM((2, NV, 16, T), BF16),
             pltpu.VMEM((NO, 2, 16, T), BF16),
         ]
-        + [sem] * 4
-        + [sem((8,))]
-        + [sem] * 9
+        + [sem] * 13
         + [sem((7,)), pltpu.SemaphoreType.REGULAR],
         compiler_params=pltpu.CompilerParams(
             collective_id=0, has_side_effects=True, vmem_limit_bytes=64 << 20
         ),
-    )(lam, drive, order, jnp.swapaxes(dom_tiles, 1, 2), dom_len, factors, e_occ, e_virt)
+    )(lam, drive, order, jnp.swapaxes(dom_tiles, 1, 2), dom_len, factors.reshape(1, 4 * T, T), e_occ, e_virt)
 
 
 def solution(mesh):

time: 41.7 us -> 40.7 us (0.976)
  Pallas kernels: 38.8 us -> 37.6 us
    pallas_call x1, Pallas kernels: 38.8 us -> 37.6 us  [shards(): pl.pallas_call(kernel, out_shape=(jax.ShapeDtypeStruct((1, NO, 8, 2 * T),...]
where the time goes in v3:
time: 40.7 us; the launch traced here: 40.3 us
  Pallas kernels  37.6 us (92%)
  local copies, waits for them, and re-layouts  2.04 us (5%)
  between operations  0.65 us (2%)
    pallas_call x1, Pallas kernels, shards(): pl.pallas_call(kernel, out_shape=(jax.ShapeDtypeStruct((1, NO, 8, 2 * T),...  37.6 us
    unnamed x4, local copies, waits for them, and re-layouts  2.04 us

profile of v3, /device:TPU:1, one launch (start us, length us, event | category | flops | bytes accessed | tf_op | source)
XLA Modules:
  0.0 40.3 jit_solution(9264630316137867674)
XLA Ops:
  0.6 37.6 %shard_map.95 = (bf16[1,16,8,256]{3,2,1,0:T(8,128)(2,1)}, f32[2,1,16]{2,1,0:T(1,128)}) custom-call(bf16[1,16,8,256]{3,2,1,0:T(8,128)(2,1)} %lam_in.1, f32[1,16,8,256]{3,2,1,0:T(8,128)} %drive_in.1, s32[1,16]{1,0:T(1,128)} %order_in.1, s32[1,2,16]{2,1,0:T(2,128)} %bitcast.3, s32[1,16]{1,0:T(1,128)} %lens_in.1, bf16[1,512,128]{2,1,0:T(8,128)(2,1)} %bitcast.2, ...), custom_call_target="tpu_custom_call" | custom-call | tf_op jit(solution)/shard_map/pallas_call | solution.py:396
  38.3 0.0 copy-start
  38.3 1.5 %copy.12 = bf16[1,16,8,256]{3,2,1,0:T(8,128)(2,1)} copy(bf16[1,16,8,256]{3,2,1,0:T(8,128)(2,1)} %get-tuple-element.4) | data formatting | bytes 131072
  39.8 0.0 copy-done
  39.8 0.6 %copy.13 = f32[2,1,16]{2,1,0:T(1,128)} copy(f32[2,1,16]{2,1,0:T(1,128)S(1)} %copy-done) | data formatting | bytes 256
Async XLA Ops:
  38.3 1.5 %copy-start = (f32[2,1,16]{2,1,0:T(1,128)S(1)}, f32[2,1,16]{2,1,0:T(1,128)}, u32[]{:S(2)}) copy-start(f32[2,1,16]{2,1,0:T(1,128)} %get-tuple-element.5) | copy-start | bytes 388

commit v4 on v3

--- a/solution.py
+++ b/solution.py
@@ -11,42 +11,24 @@
 MESH = pl.DeviceIdType.MESH
 NZ, NV, NO, T = 8, 32, 16, 128
 Y_ORDER = (4, 3, 5, 2, 6, 1, 7)
-X_ORDER = (2, 1, 3)
-
-
-def host_of(z, c, d, cj, ty):
-    if d == 0:
-        diag = c == cj
-        g = jnp.where(diag, 1, 0)
-        t = jnp.where(diag, c, ty)
-        return z, 2 * g + t, jnp.where(diag, ty, c)
-    if d < 4:
-        zh = lax.rem(z + (d >= 2), NZ) if d >= 2 else z
-        return zh, 2 * (2 + 4 * (d - 1) + 2 * c + cj) + ty, 0
-    if d > 4:
-        e = NZ - d
-        zh = lax.rem(z + d + (e >= 2), NZ)
-        return zh, 2 * (2 + 4 * (e - 1) + 2 * cj + c) + ty, 1
-    low = z < 4
-    c_low, c_high = jnp.where(low, c, cj), jnp.where(low, cj, c)
-    zh = lax.rem(lax.rem(z, 4) + 2 + 4 * c_low, NZ)
-    return zh, 2 * (14 + c_high) + ty, jnp.where(low, 0, 1)
-
-
-def pair_of(zh, v):
-    g, t = lax.div(v, 2), lax.rem(v, 2)
-    b = jnp.maximum(g - 2, 0)
-    d = lax.div(b, 4) + 1
-    z_mid = lax.rem(zh + NZ - jnp.where(d >= 2, 1, 0), NZ)
-    i_mid = 2 * z_mid + lax.rem(lax.div(b, 2), 2)
-    j_mid = 2 * lax.rem(z_mid + d, NZ) + lax.rem(b, 2)
-    zl = lax.rem(zh + 6, NZ)
-    z_far = lax.rem(zl, 4)
-    i_far = 2 * z_far + lax.div(zl, 4)
-    j_far = 2 * (z_far + 4) + (g - 14)
-    i = jnp.where(g == 0, 2 * zh, jnp.where(g == 1, 2 * zh + t, jnp.where(g >= 14, i_far, i_mid)))
-    j = jnp.where(g == 0, 2 * zh + 1, jnp.where(g == 1, 2 * zh + t, jnp.where(g >= 14, j_far, j_mid)))
-    return i, j
+
+
+def host_of(i, j, ty):
+    diag = i == j
+    low, high = jnp.minimum(i, j), jnp.maximum(i, j)
+    rank = lax.div(low * (31 - low), 2) + high - low - 1
+    plane = jnp.where(diag, lax.div(i, 2), lax.div(rank, 15))
+    virt = jnp.where(diag, lax.rem(i, 2), 2 + 2 * lax.rem(rank, 15) + ty)
+    return plane, virt, jnp.where(diag, ty, (i > j).astype(I32))
+
+
+def pair_of(plane, v):
+    g = lax.div(v, 2)
+    rank = 15 * plane + jnp.maximum(g - 1, 0)
+    low = sum((rank >= n * (31 - n) // 2).astype(I32) for n in range(1, 15))
+    high = rank - lax.div(low * (31 - low), 2) + low + 1
+    own = 2 * plane + lax.rem(v, 2)
+    return jnp.where(g == 0, own, low), jnp.where(g == 0, own, high)
 
 
 def kernel(
@@ -54,7 +36,7 @@
     out, norms,
     lam, drive, order, tiles, lens, e_occ, e_virt,
     send, recv, buf1, sel, buf2, ev_own, evb, tab_own, tab, tab_s, ids, cur, drv, den, inv, osend, orecv,
-    s_amp, r_amp, s_fac, r_fac, s_ev, r_ev, s_tab, r_tab, s_sel, r_sel, s_out, r_out, l_sem, in_sems, go,
+    s_amp, r_amp, s_fac, r_fac, s_ev, r_ev, s_tab, r_tab, s_sel, r_sel, s_out, r_out, l_sem, in_sems, column, ready,
 ):
     p, v = lax.axis_index("pair"), lax.axis_index("virt")
     z, c = lax.div(p, 2), lax.rem(p, 2)
@@ -63,7 +45,7 @@
     host = c == 1
     my_i, my_j = pair_of(z, v)
     my_t = lax.rem(v, 2)
-    diag = lax.div(v, 2) == 1
+    diag = lax.div(v, 2) == 0
     row_1 = jnp.where(diag, my_i, my_j)
 
     def remote(src, dst, ss, rs, pp, vv):
@@ -106,23 +88,17 @@
             greet(p, far_first(step))
 
         for dz in Y_ORDER:
-            greet(at_z(dz), v)
             greet(at_z(dz) - 1, v)
         greet(p - 1, v)
 
     targets = []
-    for d in range(NZ):
-        for cj in range(2):
-            for h in range(2):
-                zh, vh, side = host_of(z, c, d, cj, lax.rem(k_own + h, 2))
-                own = jnp.logical_and(host, vh == v) if d < 2 else None
-                targets.append((2 * d + cj, h, 2 * zh + 1, vh, side, own))
+    for j in range(NO):
+        for h in range(2):
+            zh, vh, side = host_of(p, j, lax.rem(k_own + h, 2))
+            targets.append((j, h, 2 * zh + 1, vh, side, jnp.logical_and(2 * zh + 1 == p, vh == v)))
 
     def away(own, act):
-        if own is None:
-            act()
-        else:
-            pl.when(jnp.logical_not(own))(act)
+        pl.when(jnp.logical_not(own))(act)
 
     for load in loads[:2]:
         load.wait()
@@ -134,11 +110,8 @@
         row_table = jnp.where(lane == 32 + j, lens[0, j], row_table)
     tab_own[...] = row_table
 
-    my_rows = 4 * z + x
-
     def slice_at(place):
-        rows = 4 * z + lax.div(place, 8)
-        return factors.at[0, pl.ds(pl.multiple_of(16 * rows, 16), 16)]
+        return factors.at[0, pl.ds(pl.multiple_of(16 * place, 16), 16)]
 
     def slice_copy(place):
         return remote(slice_at(place), buf1.at[v], s_fac, r_fac, p, place)
@@ -146,11 +119,12 @@
     def tab_copy(dz):
         return remote(tab_own, tab.at[p], s_tab, r_tab, at_z(dz), v)
 
+    def tell(sem, pp):
+        pl.semaphore_signal(sem, inc=1, device_id={"pair": pp, "virt": v}, device_id_type=MESH)
+
     @pl.when(host)
     def _():
-        pl.semaphore_wait(barrier, NV - 1 + NZ - 1)
-        for dz in Y_ORDER:
-            tab_copy(dz).start()
+        pl.semaphore_wait(barrier, NV - 1)
 
         @pl.loop(0, NV - 1)
         def _(step):
@@ -162,6 +136,7 @@
     @pl.when(jnp.logical_not(host))
     def _():
         pl.semaphore_wait(barrier, NZ)
+        tell(column, p + 1)
         for dz in Y_ORDER:
             tab_copy(dz).start()
         tab_copy(0).start()
@@ -173,7 +148,7 @@
     def find(s, found):
         o = order[0, s]
         return tuple(
-            jnp.where(o == 2 * lax.rem(z + n // 2, NZ) + n % 2, s, f) for n, f in enumerate(found)
+            jnp.where(o == n, s, f) for n, f in enumerate(found)
         )
 
     slots = lax.fori_loop(0, NO, find, (jnp.int32(0),) * NO)
@@ -186,12 +161,17 @@
 
     @pl.when(host)
     def _():
-        drain(tab, r_tab)
-        pl.semaphore_signal(go, inc=1, device_id={"pair": p - 1, "virt": v}, device_id_type=MESH)
+        pl.semaphore_wait(column, 1)
+        for dz in Y_ORDER:
+            tell(ready, at_z(dz))
+        for dz in Y_ORDER:
+            tab_copy(dz).start()
+        pl.semaphore_wait(ready, NZ - 1)
+        tell(ready, p - 1)
 
     @pl.when(jnp.logical_not(host))
     def _():
-        pl.semaphore_wait(go, 1)
+        pl.semaphore_wait(ready, 1)
 
     def amp_copy(n, h, side, pp, vv):
         return remote(send.at[n, h], recv.at[side, v], s_amp, r_amp, pp, vv)
@@ -200,11 +180,7 @@
         return remote(ev_own, evb.at[v], s_ev, r_ev, pp, vv)
 
     def when_first(side, act):
-        if isinstance(side, int):
-            if side == 0:
-                act()
-        else:
-            pl.when(side == 0)(act)
+        pl.when(side == 0)(act)
 
     for n, h, pp, vv, side, own in targets:
         def send_away():
@@ -212,33 +188,38 @@
             when_first(side, lambda: ev_copy(pp, vv).start())
 
         away(own, send_away)
-        if own is not None:
-            @pl.when(own)
-            def _():
-                pltpu.make_async_copy(send.at[n, h], recv.at[side, v], r_amp).start()
-                when_first(side, lambda: pltpu.make_async_copy(ev_own, evb.at[v], r_ev).start())
+
+        @pl.when(own)
+        def _():
+            pltpu.make_async_copy(send.at[n, h], recv.at[side, v], r_amp).start()
+            when_first(side, lambda: pltpu.make_async_copy(ev_own, evb.at[v], r_ev).start())
 
     @pl.when(host)
     def _():
+        drain(tab, r_tab)
         to_smem = pltpu.make_async_copy(tab, tab_s, l_sem)
         to_smem.start()
         to_smem.wait()
-        places = [
-            (lax.rem(z + dz, NZ), 8 * lax.rem(x + dx, 4) + y) for dz in Y_ORDER + (0,) for dx in X_ORDER + (0,)
-        ]
-        for n, (zd, vd) in enumerate(places):
-            i, j = pair_of(zd, vd)
+
+        @pl.loop(0, NV)
+        def _(w):
+            i, j = pair_of(z, w)
             for k in range(2):
-                ids[2 * n + k] = tab_s[i, 0, 2 * j + k]
-        own_tiles = [ids[62 + k] for k in range(2)]
+                ids[2 * w + k] = tab_s[i, 0, 2 * j + k]
+
+        own_tiles = [ids[2 * v + k] for k in range(2)]
         drain(buf1, r_fac)
-        for n, (zd, vd) in enumerate(places):
+
+        @pl.loop(0, NV - 1)
+        def _(step):
+            w = far_first(step)
             for k in range(2):
-                sel[n, k] = buf1[ids[2 * n + k]]
-            if n < 31:
-                remote(sel.at[n], buf2.at[:, my_rows], s_sel, r_sel, 2 * zd + 1, vd).start()
-            else:
-                pltpu.make_async_copy(sel.at[n], buf2.at[:, my_rows], r_sel).start()
+                sel[w, k] = buf1[ids[2 * w + k]]
+            remote(sel.at[w], buf2.at[:, v], s_sel, r_sel, p, w).start()
+
+        for k in range(2):
+            sel[v, k] = buf1[own_tiles[k]]
+        pltpu.make_async_copy(sel.at[v], buf2.at[:, v], r_sel).start()
         length = tab_s[my_i, 0, 32 + my_j]
         occ = e_occ[my_i] + e_occ[my_j]
         drain(evb, r_ev)
@@ -428,7 +409,7 @@
             pltpu.VMEM((NO, 2, 16, T), BF16),
         ]
         + [sem] * 13
-        + [sem((7,)), pltpu.SemaphoreType.REGULAR],
+        + [sem((7,)), pltpu.SemaphoreType.REGULAR, pltpu.SemaphoreType.REGULAR],
         compiler_params=pltpu.CompilerParams(
             collective_id=0, has_side_effects=True, vmem_limit_bytes=64 << 20
         ),

time: 40.7 us -> 38.9 us (0.956)
  Pallas kernels: 37.6 us -> 36.1 us
    pallas_call x1, Pallas kernels: 37.6 us -> 36.1 us  [shards(): pl.pallas_call(kernel, out_shape=(jax.ShapeDtypeStruct((1, NO, 8, 2 * T),...]
where the time goes in v4:
time: 38.9 us; the launch traced here: 38.8 us
  Pallas kernels  36.1 us (93%)
  local copies, waits for them, and re-layouts  2.04 us (5%)
  between operations  0.65 us (2%)
    pallas_call x1, Pallas kernels, shards(): pl.pallas_call(kernel, out_shape=(jax.ShapeDtypeStruct((1, NO, 8, 2 * T),...  36.1 us
    unnamed x4, local copies, waits for them, and re-layouts  2.04 us

profile of v4, /device:TPU:1, one launch (start us, length us, event | category | flops | bytes accessed | tf_op | source)
XLA Modules:
  0.0 38.8 jit_solution(12053300470989518827)
XLA Ops:
  0.6 36.1 %shard_map.95 = (bf16[1,16,8,256]{3,2,1,0:T(8,128)(2,1)}, f32[2,1,16]{2,1,0:T(1,128)}) custom-call(bf16[1,16,8,256]{3,2,1,0:T(8,128)(2,1)} %lam_in.1, f32[1,16,8,256]{3,2,1,0:T(8,128)} %drive_in.1, s32[1,16]{1,0:T(1,128)} %order_in.1, s32[1,2,16]{2,1,0:T(2,128)} %bitcast.3, s32[1,16]{1,0:T(1,128)} %lens_in.1, bf16[1,512,128]{2,1,0:T(8,128)(2,1)} %bitcast.2, ...), custom_call_target="tpu_custom_call" | custom-call | tf_op jit(solution)/shard_map/pallas_call | solution.py:377
  36.7 0.0 copy-start
  36.7 1.5 %copy.12 = bf16[1,16,8,256]{3,2,1,0:T(8,128)(2,1)} copy(bf16[1,16,8,256]{3,2,1,0:T(8,128)(2,1)} %get-tuple-element.4) | data formatting | bytes 131072
  38.2 0.0 copy-done
  38.2 0.6 %copy.13 = f32[2,1,16]{2,1,0:T(1,128)} copy(f32[2,1,16]{2,1,0:T(1,128)S(1)} %copy-done) | data formatting | bytes 256
Async XLA Ops:
  36.7 1.5 %copy-start = (f32[2,1,16]{2,1,0:T(1,128)S(1)}, f32[2,1,16]{2,1,0:T(1,128)}, u32[]{:S(2)}) copy-start(f32[2,1,16]{2,1,0:T(1,128)} %get-tuple-element.5) | copy-start | bytes 388

commit v5 on v4

--- a/solution.py
+++ b/solution.py
@@ -33,9 +33,9 @@
 
 def kernel(
     lam_in, drive_in, order_in, tiles_in, lens_in, factors, e_occ_in, e_virt_in,
-    out, norms,
+    orecv,
     lam, drive, order, tiles, lens, e_occ, e_virt,
-    send, recv, buf1, sel, buf2, ev_own, evb, tab_own, tab, tab_s, ids, cur, drv, den, inv, osend, orecv,
+    send, recv, buf1, sel, buf2, ev_own, evb, tab_own, tab, tab_s, pairs, cur, drv, den, inv, osend,
     s_amp, r_amp, s_fac, r_fac, s_ev, r_ev, s_tab, r_tab, s_sel, r_sel, s_out, r_out, l_sem, in_sems, column, ready,
 ):
     p, v = lax.axis_index("pair"), lax.axis_index("virt")
@@ -64,8 +64,7 @@
             (e_virt_in, e_virt), (e_occ_in, e_occ),
         ])
     ]
-    for load in loads:
-        load.start()
+    tab[...] = jnp.zeros_like(tab)
 
     barrier = pltpu.get_barrier_semaphore()
 
@@ -75,21 +74,20 @@
     def at_z(dz):
         return 2 * lax.rem(z + dz, NZ) + 1
 
-    def far_first(step):
-        a, b = lax.div(step, 4), lax.rem(step, 4)
-        dy = jnp.where(lax.rem(a, 2) == 1, 4 - lax.div(a + 1, 2), 4 + lax.div(a, 2))
-        dx = jnp.where(lax.rem(b, 2) == 1, 2 - lax.div(b + 1, 2), 2 + lax.div(b, 2))
-        return 8 * lax.rem(x + dx, 4) + lax.rem(y + dy, 8)
-
-    @pl.when(host)
-    def _():
-        @pl.loop(0, NV - 1)
-        def _(step):
-            greet(p, far_first(step))
-
+    at_x = [8 * lax.rem(x + dx, 4) for dx in range(4)]
+    at_y = [lax.rem(y + dy, 8) for dy in range(8)]
+    places = [at_x[dx] + at_y[dy] for dy in Y_ORDER + (0,) for dx in (2, 1, 3, 0)][:-1]
+
+    @pl.when(host)
+    def _():
+        for place in places:
+            greet(p, place)
         for dz in Y_ORDER:
             greet(at_z(dz) - 1, v)
         greet(p - 1, v)
+
+    for load in loads:
+        load.start()
 
     targets = []
     for j in range(NO):
@@ -99,6 +97,14 @@
 
     def away(own, act):
         pl.when(jnp.logical_not(own))(act)
+
+    @pl.when(host)
+    def _():
+        @pl.loop(0, NV)
+        def _(w):
+            i, j = pair_of(z, w)
+            pairs[2 * w] = i
+            pairs[2 * w + 1] = 2 * j
 
     for load in loads[:2]:
         load.wait()
@@ -116,30 +122,21 @@
     def slice_copy(place):
         return remote(slice_at(place), buf1.at[v], s_fac, r_fac, p, place)
 
+    def ev_copy(place):
+        return remote(ev_own, evb.at[v], s_ev, r_ev, p, place)
+
     def tab_copy(dz):
         return remote(tab_own, tab.at[p], s_tab, r_tab, at_z(dz), v)
 
+    def near_tables(dz, act):
+        pl.when(z + dz < NZ)(lambda: act(tab_copy(dz)))
+
+    def send_tables(first):
+        for dz in range(first, 4):
+            near_tables(dz, lambda copy: copy.start())
+
     def tell(sem, pp):
         pl.semaphore_signal(sem, inc=1, device_id={"pair": pp, "virt": v}, device_id_type=MESH)
-
-    @pl.when(host)
-    def _():
-        pl.semaphore_wait(barrier, NV - 1)
-
-        @pl.loop(0, NV - 1)
-        def _(step):
-            slice_copy(far_first(step)).start()
-
-        pltpu.make_async_copy(slice_at(v), buf1.at[v], r_fac).start()
-        pltpu.make_async_copy(tab_own, tab.at[p], r_tab).start()
-
-    @pl.when(jnp.logical_not(host))
-    def _():
-        pl.semaphore_wait(barrier, NZ)
-        tell(column, p + 1)
-        for dz in Y_ORDER:
-            tab_copy(dz).start()
-        tab_copy(0).start()
 
     for load in loads[2:]:
         load.wait()
@@ -161,11 +158,51 @@
 
     @pl.when(host)
     def _():
+        pl.semaphore_wait(barrier, NV - 1)
+
+        for place in places:
+            slice_copy(place).start()
+        for place in places:
+            ev_copy(place).start()
+        pltpu.make_async_copy(slice_at(v), buf1.at[v], r_fac).start()
+        pltpu.make_async_copy(ev_own, evb.at[v], r_ev).start()
+        pltpu.make_async_copy(tab_own, tab.at[p], r_tab).start()
+
+    @pl.when(jnp.logical_not(host))
+    def _():
+        pl.semaphore_wait(barrier, NZ)
+        tell(column, p + 1)
+        send_tables(0)
+
+    def tile(w, k):
+        return tab_s[pairs[2 * w], 0, pairs[2 * w + 1] + k]
+
+    def send_slices():
+        drain(buf1, r_fac)
+        for w in places:
+            for k in range(2):
+                sel[w, k] = buf1[tile(w, k)]
+            remote(sel.at[w], buf2.at[:, v], s_sel, r_sel, p, w).start()
+        for k in range(2):
+            sel[v, k] = buf1[tile(v, k)]
+        pltpu.make_async_copy(sel.at[v], buf2.at[:, v], r_sel).start()
+
+    early = z < 4
+
+    @pl.when(host)
+    def _():
         pl.semaphore_wait(column, 1)
         for dz in Y_ORDER:
             tell(ready, at_z(dz))
-        for dz in Y_ORDER:
-            tab_copy(dz).start()
+        send_tables(1)
+        for n in range(1, 5):
+            @pl.when(jnp.minimum(z, 3) + 1 == n)
+            def _():
+                drain(tab.at[0 : 2 * n], r_tab)
+        to_smem = pltpu.make_async_copy(tab, tab_s, l_sem)
+        to_smem.start()
+        to_smem.wait()
+        pl.when(early)(send_slices)
         pl.semaphore_wait(ready, NZ - 1)
         tell(ready, p - 1)
 
@@ -176,50 +213,17 @@
     def amp_copy(n, h, side, pp, vv):
         return remote(send.at[n, h], recv.at[side, v], s_amp, r_amp, pp, vv)
 
-    def ev_copy(pp, vv):
-        return remote(ev_own, evb.at[v], s_ev, r_ev, pp, vv)
-
-    def when_first(side, act):
-        pl.when(side == 0)(act)
-
     for n, h, pp, vv, side, own in targets:
-        def send_away():
-            amp_copy(n, h, side, pp, vv).start()
-            when_first(side, lambda: ev_copy(pp, vv).start())
-
-        away(own, send_away)
+        away(own, lambda: amp_copy(n, h, side, pp, vv).start())
 
         @pl.when(own)
         def _():
             pltpu.make_async_copy(send.at[n, h], recv.at[side, v], r_amp).start()
-            when_first(side, lambda: pltpu.make_async_copy(ev_own, evb.at[v], r_ev).start())
-
-    @pl.when(host)
-    def _():
-        drain(tab, r_tab)
-        to_smem = pltpu.make_async_copy(tab, tab_s, l_sem)
-        to_smem.start()
-        to_smem.wait()
-
-        @pl.loop(0, NV)
-        def _(w):
-            i, j = pair_of(z, w)
-            for k in range(2):
-                ids[2 * w + k] = tab_s[i, 0, 2 * j + k]
-
-        own_tiles = [ids[2 * v + k] for k in range(2)]
-        drain(buf1, r_fac)
-
-        @pl.loop(0, NV - 1)
-        def _(step):
-            w = far_first(step)
-            for k in range(2):
-                sel[w, k] = buf1[ids[2 * w + k]]
-            remote(sel.at[w], buf2.at[:, v], s_sel, r_sel, p, w).start()
-
-        for k in range(2):
-            sel[v, k] = buf1[own_tiles[k]]
-        pltpu.make_async_copy(sel.at[v], buf2.at[:, v], r_sel).start()
+
+    @pl.when(host)
+    def _():
+        pl.when(jnp.logical_not(early))(send_slices)
+        own_tiles = [tile(v, k) for k in range(2)]
         length = tab_s[my_i, 0, 32 + my_j]
         occ = e_occ[my_i] + e_occ[my_j]
         drain(evb, r_ev)
@@ -328,13 +332,9 @@
                     pltpu.make_async_copy(osend.at[s, w], dst, r_out).start()
 
     for n, h, pp, vv, side, own in targets:
-        def left():
-            amp_copy(n, h, side, pp, vv).wait_send()
-            when_first(side, lambda: ev_copy(pp, vv).wait_send())
-
-        away(own, left)
-    for dz in range(1, NZ):
-        tab_copy(dz).wait_send()
+        away(own, lambda: amp_copy(n, h, side, pp, vv).wait_send())
+    for dz in range(1, 4):
+        near_tables(dz, lambda copy: copy.wait_send())
 
     @pl.when(jnp.logical_not(host))
     def _():
@@ -343,6 +343,7 @@
     @pl.when(host)
     def _():
         drain(buf1.at[0 : NV - 1], s_fac)
+        drain(evb.at[0 : NV - 1], s_ev)
         drain(sel.at[0 : NV - 1], s_sel)
         for s in range(2):
             row = my_i if s == 0 else row_1
@@ -354,6 +355,10 @@
                     remote(osend.at[s, w], osend.at[s, w], s_out, r_out, row, w).wait_send()
 
     drain(orecv, r_out)
+
+
+def unpack(orecv, order, lens, out, norms):
+    lane = lax.broadcasted_iota(I32, (1, T), 1)
     totals = [jnp.zeros((1, T), F32), jnp.zeros((1, T), F32)]
     count = jnp.ones((1, T), F32)
     for s in range(NO):
@@ -372,16 +377,14 @@
 
 
 def shards(lam, drive, order, dom_tiles, dom_len, factors, e_occ, e_virt):
-    vmem = pl.BlockSpec(memory_space=pltpu.VMEM)
+    vmem, smem = pl.BlockSpec(memory_space=pltpu.VMEM), pl.BlockSpec(memory_space=pltpu.SMEM)
+    hbm = pl.BlockSpec(memory_space=pltpu.HBM)
     sem = pltpu.SemaphoreType.DMA
-    return pl.pallas_call(
+    pieces = pl.pallas_call(
         kernel,
-        out_shape=(
-            jax.ShapeDtypeStruct((1, NO, 8, 2 * T), BF16),
-            jax.ShapeDtypeStruct((2, 1, NO), F32),
-        ),
-        in_specs=[pl.BlockSpec(memory_space=pltpu.HBM)] * 8,
-        out_specs=(vmem, vmem),
+        out_shape=jax.ShapeDtypeStruct((NO, 2, 16, T), BF16),
+        in_specs=[hbm] * 8,
+        out_specs=hbm,
         scratch_shapes=[
             pltpu.VMEM((1, NO, 8, 2 * T), BF16),
             pltpu.VMEM((1, NO, 8, 2 * T), F32),
@@ -406,7 +409,6 @@
             pltpu.VMEM((3, T, T), F32),
             pltpu.VMEM((3, T, T), F32),
             pltpu.VMEM((2, NV, 16, T), BF16),
-            pltpu.VMEM((NO, 2, 16, T), BF16),
         ]
         + [sem] * 13
         + [sem((7,)), pltpu.SemaphoreType.REGULAR, pltpu.SemaphoreType.REGULAR],
@@ -414,6 +416,16 @@
             collective_id=0, has_side_effects=True, vmem_limit_bytes=64 << 20
         ),
     )(lam, drive, order, jnp.swapaxes(dom_tiles, 1, 2), dom_len, factors.reshape(1, 4 * T, T), e_occ, e_virt)
+    return pl.pallas_call(
+        unpack,
+        out_shape=(
+            jax.ShapeDtypeStruct((1, NO, 8, 2 * T), BF16),
+            jax.ShapeDtypeStruct((2, 1, NO), F32),
+        ),
+        in_specs=[vmem, smem, smem],
+        out_specs=(vmem, vmem),
+        compiler_params=pltpu.CompilerParams(vmem_limit_bytes=64 << 20),
+    )(pieces, order, dom_len)
 
 
 def solution(mesh):

time: 38.9 us -> 36.9 us (0.949)
  the two profiles are of different devices: /device:TPU:1 before, /device:TPU:7 now
where the time goes in v5:
time: 36.9 us; the launch traced here: 36.7 us
  Pallas kernels  36.1 us (98%)
  between operations  0.64 us (2%)
    pallas_call x1, Pallas kernels, shards(): pl.pallas_call(kernel, out_shape=jax.ShapeDtypeStruct((NO, 2, 16, T), BF1...  34.5 us
    pallas_call x1, Pallas kernels, shards(): pl.pallas_call(unpack, out_shape=(jax.ShapeDtypeStruct((1, NO, 8, 2 * T),...  1.58 us

profile of v5, /device:TPU:7, one launch (start us, length us, event | category | flops | bytes accessed | tf_op | source)
XLA Modules:
  0.0 36.7 jit_solution(8549599630237754542)
XLA Ops:
  0.6 34.5 %shard_map.95.orecv = bf16[16,2,16,128]{3,2,1,0:T(8,128)(2,1)} custom-call(bf16[1,16,8,256]{3,2,1,0:T(8,128)(2,1)} %lam_in.1, f32[1,16,8,256]{3,2,1,0:T(8,128)} %drive_in.1, s32[1,16]{1,0:T(1,128)} %order.1, s32[1,2,16]{2,1,0:T(2,128)} %bitcast.3, s32[1,16]{1,0:T(1,128)} %lens.1, bf16[1,512,128]{2,1,0:T(8,128)(2,1)} %bitcast.2, f32[16]{0:T(128)} %e_occ_in.1, ...), custom_call_target="tpu_custom_call" | custom-call | tf_op jit(solution)/shard_map/pallas_call | solution.py:383
  35.2 1.6 %shard_map.96 = (bf16[1,16,8,256]{3,2,1,0:T(8,128)(2,1)}, f32[2,1,16]{2,1,0:T(1,128)}) custom-call(bf16[16,2,16,128]{3,2,1,0:T(8,128)(2,1)} %shard_map.95.orecv, s32[1,16]{1,0:T(1,128)} %order.1, s32[1,16]{1,0:T(1,128)} %lens.1), custom_call_target="tpu_custom_call" | custom-call | tf_op jit(solution)/shard_map/pallas_call | solution.py:419

commit v6 on v5

--- a/solution.py
+++ b/solution.py
@@ -10,6 +10,7 @@
 F32, BF16, I32 = jnp.float32, jnp.bfloat16, jnp.int32
 MESH = pl.DeviceIdType.MESH
 NZ, NV, NO, T = 8, 32, 16, 128
+EARLY = 4
 Y_ORDER = (4, 3, 5, 2, 6, 1, 7)
 
 
@@ -47,6 +48,7 @@
     my_t = lax.rem(v, 2)
     diag = lax.div(v, 2) == 0
     row_1 = jnp.where(diag, my_i, my_j)
+    early = z < EARLY
 
     def remote(src, dst, ss, rs, pp, vv):
         return pltpu.make_async_remote_copy(
@@ -86,6 +88,13 @@
             greet(at_z(dz) - 1, v)
         greet(p - 1, v)
 
+        @pl.when(early)
+        def _():
+            @pl.loop(0, NV)
+            def _(w):
+                for row in (my_i, row_1):
+                    greet(2 * lax.div(row, 2), w)
+
     for load in loads:
         load.start()
 
@@ -93,7 +102,12 @@
     for j in range(NO):
         for h in range(2):
             zh, vh, side = host_of(p, j, lax.rem(k_own + h, 2))
-            targets.append((j, h, 2 * zh + 1, vh, side, jnp.logical_and(2 * zh + 1 == p, vh == v)))
+            own = jnp.logical_and(2 * zh + 1 == p, vh == v)
+            targets.append((j, h, 2 * zh + 1, vh, side, own, zh < EARLY))
+    greetings = NZ
+    for j in range(NO):
+        for row in range(2):
+            greetings += 2 * (host_of(2 * z + row, j, 0)[0] < EARLY).astype(I32)
 
     def away(own, act):
         pl.when(jnp.logical_not(own))(act)
@@ -156,6 +170,21 @@
             cols = slice(h * T, (h + 1) * T)
             send[n, h] = jnp.concatenate([own_lam[:, cols], own_drive[:, cols]], axis=0).astype(BF16)
 
+    def amp_copy(n, h, side, pp, vv):
+        return remote(send.at[n, h], recv.at[side, v], s_amp, r_amp, pp, vv)
+
+    def send_amplitudes(to_early):
+        for n, h, pp, vv, side, own, at_early in targets:
+            now = at_early if to_early else jnp.logical_not(at_early)
+
+            @pl.when(jnp.logical_and(now, jnp.logical_not(own)))
+            def _():
+                amp_copy(n, h, side, pp, vv).start()
+
+            @pl.when(jnp.logical_and(now, own))
+            def _():
+                pltpu.make_async_copy(send.at[n, h], recv.at[side, v], r_amp).start()
+
     @pl.when(host)
     def _():
         pl.semaphore_wait(barrier, NV - 1)
@@ -170,9 +199,10 @@
 
     @pl.when(jnp.logical_not(host))
     def _():
-        pl.semaphore_wait(barrier, NZ)
+        pl.semaphore_wait(barrier, greetings)
         tell(column, p + 1)
         send_tables(0)
+        send_amplitudes(True)
 
     def tile(w, k):
         return tab_s[pairs[2 * w], 0, pairs[2 * w + 1] + k]
@@ -187,14 +217,13 @@
             sel[v, k] = buf1[tile(v, k)]
         pltpu.make_async_copy(sel.at[v], buf2.at[:, v], r_sel).start()
 
-    early = z < 4
-
     @pl.when(host)
     def _():
         pl.semaphore_wait(column, 1)
         for dz in Y_ORDER:
             tell(ready, at_z(dz))
         send_tables(1)
+        send_amplitudes(True)
         for n in range(1, 5):
             @pl.when(jnp.minimum(z, 3) + 1 == n)
             def _():
@@ -210,15 +239,7 @@
     def _():
         pl.semaphore_wait(ready, 1)
 
-    def amp_copy(n, h, side, pp, vv):
-        return remote(send.at[n, h], recv.at[side, v], s_amp, r_amp, pp, vv)
-
-    for n, h, pp, vv, side, own in targets:
-        away(own, lambda: amp_copy(n, h, side, pp, vv).start())
-
-        @pl.when(own)
-        def _():
-            pltpu.make_async_copy(send.at[n, h], recv.at[side, v], r_amp).start()
+    send_amplitudes(False)
 
     @pl.when(host)
     def _():
@@ -331,7 +352,7 @@
                 def _():
                     pltpu.make_async_copy(osend.at[s, w], dst, r_out).start()
 
-    for n, h, pp, vv, side, own in targets:
+    for n, h, pp, vv, side, own, _ in targets:
         away(own, lambda: amp_copy(n, h, side, pp, vv).wait_send())
     for dz in range(1, 4):
         near_tables(dz, lambda copy: copy.wait_send())

time: 36.9 us -> 35.1 us (0.951)
  the two profiles are of different devices: /device:TPU:7 before, /device:TPU:1 now
where the time goes in v6:
time: 35.1 us; the launch traced here: 34.6 us
  Pallas kernels  34 us (97%)
  between operations  0.64 us (2%)
    pallas_call x1, Pallas kernels, shards(): pl.pallas_call(kernel, out_shape=jax.ShapeDtypeStruct((NO, 2, 16, T), BF1...  32.4 us
    pallas_call x1, Pallas kernels, shards(): pl.pallas_call(unpack, out_shape=(jax.ShapeDtypeStruct((1, NO, 8, 2 * T),...  1.58 us

profile of v6, /device:TPU:1, one launch (start us, length us, event | category | flops | bytes accessed | tf_op | source)
XLA Modules:
  0.0 34.6 jit_solution(11129988794849564733)
XLA Ops:
  0.6 32.4 %shard_map.95.orecv = bf16[16,2,16,128]{3,2,1,0:T(8,128)(2,1)} custom-call(bf16[1,16,8,256]{3,2,1,0:T(8,128)(2,1)} %lam_in.1, f32[1,16,8,256]{3,2,1,0:T(8,128)} %drive_in.1, s32[1,16]{1,0:T(1,128)} %order.1, s32[1,2,16]{2,1,0:T(2,128)} %bitcast.3, s32[1,16]{1,0:T(1,128)} %lens.1, bf16[1,512,128]{2,1,0:T(8,128)(2,1)} %bitcast.2, f32[16]{0:T(128)} %e_occ_in.1, ...), custom_call_target="tpu_custom_call" | custom-call | tf_op jit(solution)/shard_map/pallas_call | solution.py:404
  33.0 1.6 %shard_map.96 = (bf16[1,16,8,256]{3,2,1,0:T(8,128)(2,1)}, f32[2,1,16]{2,1,0:T(1,128)}) custom-call(bf16[16,2,16,128]{3,2,1,0:T(8,128)(2,1)} %shard_map.95.orecv, s32[1,16]{1,0:T(1,128)} %order.1, s32[1,16]{1,0:T(1,128)} %lens.1), custom_call_target="tpu_custom_call" | custom-call | tf_op jit(solution)/shard_map/pallas_call | solution.py:440

commit v7 on v6

--- a/solution.py
+++ b/solution.py
@@ -231,7 +231,7 @@
         to_smem = pltpu.make_async_copy(tab, tab_s, l_sem)
         to_smem.start()
         to_smem.wait()
-        pl.when(early)(send_slices)
+        pl.when(z < 2)(send_slices)
         pl.semaphore_wait(ready, NZ - 1)
         tell(ready, p - 1)
 
@@ -243,14 +243,13 @@
 
     @pl.when(host)
     def _():
-        pl.when(jnp.logical_not(early))(send_slices)
+        pl.when(z >= 2)(send_slices)
         own_tiles = [tile(v, k) for k in range(2)]
         length = tab_s[my_i, 0, 32 + my_j]
         occ = e_occ[my_i] + e_occ[my_j]
         drain(evb, r_ev)
         e_row = [evb[tile] for tile in own_tiles]
         e_col = [jnp.transpose(jnp.broadcast_to(e, (T, T))) for e in e_row]
-        drain(recv, r_amp)
 
         crossed = jnp.logical_and(jnp.logical_not(diag), my_t == 1)
         couples = [
@@ -261,6 +260,13 @@
 
         def alive(pk, l):
             return jnp.logical_and(pk < length, l < length)
+
+        def divide(o):
+            ps, pk, qs, l = couples[o]
+            e_l = jnp.where(l == 0, e_row[0], e_row[1])
+            gap = e_col[pk] + e_l - occ
+            den[o] = gap
+            inv[o] = 1.0 / gap
 
         def prepare(o):
             ps, pk, qs, l = couples[o]
@@ -271,9 +277,6 @@
             cur[o, 1] = jnp.where(live, jnp.transpose(second[:, 0].reshape(T, T)), 0.0)
             drv[o, 0] = first[:, 1].reshape(T, T)
             drv[o, 1] = jnp.transpose(second[:, 1].reshape(T, T))
-            e_l = jnp.where(l == 0, e_row[0], e_row[1])
-            den[o] = e_col[pk] + e_l - occ
-            inv[o] = 1.0 / den[o]
 
         def iterate(o):
             ps, pk, qs, l = couples[o]
@@ -296,14 +299,14 @@
                     target = drv[o, n] + ladder
                     resid = jnp.where(live, target - den[o] * now[n], 0.0)
                     now[n] = jnp.where(live, target * inv[o], 0.0).astype(BF16).astype(F32)
-                    squares.append(jnp.sum(resid * resid, keepdims=True))
+                    squares.append(jnp.sum(resid * resid, axis=0, keepdims=True))
             return now[0], jnp.transpose(now[1]), squares
 
         def norm_rows(first, second):
             rows = jnp.zeros((8, T), F32)
             sub = lax.broadcasted_iota(I32, (8, T), 0)
             for it, total in enumerate((first, second)):
-                total = jnp.broadcast_to(total, (8, T))
+                total = jnp.broadcast_to(jnp.sum(total, axis=1, keepdims=True), (8, T))
                 high = total.astype(BF16).astype(F32)
                 rows = jnp.where(sub == 2 * it, high, jnp.where(sub == 2 * it + 1, total - high, rows))
             return jnp.broadcast_to(rows[None], (16, 8, T))
@@ -312,6 +315,9 @@
             message = jnp.concatenate([values.reshape(16, 8, T), rows], axis=1)
             osend[side, pl.ds(16 * block, 16)] = message.astype(BF16)
 
+        for o in range(3):
+            divide(o)
+        drain(recv, r_amp)
         for o in range(2):
             prepare(o)
         pl.when(diag)(lambda: prepare(2))

time: 35.1 us -> 35 us (level)
  no operation moved by 1% of the time
where the time goes in v7:
time: 35 us; the launch traced here: 34.5 us
  Pallas kernels  33.9 us (97%)
  between operations  0.64 us (2%)
    pallas_call x1, Pallas kernels, shards(): pl.pallas_call(kernel, out_shape=jax.ShapeDtypeStruct((NO, 2, 16, T), BF1...  32.3 us
    pallas_call x1, Pallas kernels, shards(): pl.pallas_call(unpack, out_shape=(jax.ShapeDtypeStruct((1, NO, 8, 2 * T),...  1.58 us

profile of v7, /device:TPU:1, one launch (start us, length us, event | category | flops | bytes accessed | tf_op | source)
XLA Modules:
  0.0 34.5 jit_solution(10556306669223513993)
XLA Ops:
  0.6 32.3 %shard_map.95.orecv = bf16[16,2,16,128]{3,2,1,0:T(8,128)(2,1)} custom-call(bf16[1,16,8,256]{3,2,1,0:T(8,128)(2,1)} %lam_in.1, f32[1,16,8,256]{3,2,1,0:T(8,128)} %drive_in.1, s32[1,16]{1,0:T(1,128)} %order.1, s32[1,2,16]{2,1,0:T(2,128)} %bitcast.3, s32[1,16]{1,0:T(1,128)} %lens.1, bf16[1,512,128]{2,1,0:T(8,128)(2,1)} %bitcast.2, f32[16]{0:T(128)} %e_occ_in.1, ...), custom_call_target="tpu_custom_call" | custom-call | tf_op jit(solution)/shard_map/pallas_call | solution.py:410
  33.0 1.6 %shard_map.96 = (bf16[1,16,8,256]{3,2,1,0:T(8,128)(2,1)}, f32[2,1,16]{2,1,0:T(1,128)}) custom-call(bf16[16,2,16,128]{3,2,1,0:T(8,128)(2,1)} %shard_map.95.orecv, s32[1,16]{1,0:T(1,128)} %order.1, s32[1,16]{1,0:T(1,128)} %lens.1), custom_call_target="tpu_custom_call" | custom-call | tf_op jit(solution)/shard_map/pallas_call | solution.py:446

commit v8 on v7

--- a/solution.py
+++ b/solution.py
@@ -344,19 +344,19 @@
         for s in range(2):
             row, col = (my_i, my_j) if s == 0 else (row_1, my_i)
 
-            @pl.loop(0, NV)
-            def _(w):
-                half = lax.rem(lax.div(w, 16) + jnp.where(diag, s, my_t), 2)
-                dst = orecv.at[col, half]
-                self_home = jnp.logical_and(row == p, w == v)
-
-                @pl.when(jnp.logical_not(self_home))
-                def _():
-                    remote(osend.at[s, w], dst, s_out, r_out, row, w).start()
-
-                @pl.when(self_home)
-                def _():
-                    pltpu.make_async_copy(osend.at[s, w], dst, r_out).start()
+            def landing(w):
+                return orecv.at[col, lax.rem(lax.div(w, 16) + jnp.where(diag, s, my_t), 2)]
+
+            for w in places:
+                remote(osend.at[s, w], landing(w), s_out, r_out, row, w).start()
+
+            @pl.when(row != p)
+            def _():
+                remote(osend.at[s, v], landing(v), s_out, r_out, row, v).start()
+
+            @pl.when(row == p)
+            def _():
+                pltpu.make_async_copy(osend.at[s, v], landing(v), r_out).start()
 
     for n, h, pp, vv, side, own, _ in targets:
         away(own, lambda: amp_copy(n, h, side, pp, vv).wait_send())

time: 35 us -> 35.3 us (level)
  no operation moved by 1% of the time
where the time goes in v8:
time: 35.3 us; the launch traced here: 34.7 us
  Pallas kernels  34 us (96%)
  between operations  0.64 us (2%)
    pallas_call x1, Pallas kernels, shards(): pl.pallas_call(kernel, out_shape=jax.ShapeDtypeStruct((NO, 2, 16, T), BF1...  32.5 us
    pallas_call x1, Pallas kernels, shards(): pl.pallas_call(unpack, out_shape=(jax.ShapeDtypeStruct((1, NO, 8, 2 * T),...  1.58 us

profile of v8, /device:TPU:1, one launch (start us, length us, event | category | flops | bytes accessed | tf_op | source)
XLA Modules:
  0.0 34.7 jit_solution(13118302654227629286)
XLA Ops:
  0.6 32.5 %shard_map.95.orecv = bf16[16,2,16,128]{3,2,1,0:T(8,128)(2,1)} custom-call(bf16[1,16,8,256]{3,2,1,0:T(8,128)(2,1)} %lam_in.1, f32[1,16,8,256]{3,2,1,0:T(8,128)} %drive_in.1, s32[1,16]{1,0:T(1,128)} %order.1, s32[1,2,16]{2,1,0:T(2,128)} %bitcast.3, s32[1,16]{1,0:T(1,128)} %lens.1, bf16[1,512,128]{2,1,0:T(8,128)(2,1)} %bitcast.2, f32[16]{0:T(128)} %e_occ_in.1, ...), custom_call_target="tpu_custom_call" | custom-call | tf_op jit(solution)/shard_map/pallas_call | solution.py:410
  33.1 1.6 %shard_map.96 = (bf16[1,16,8,256]{3,2,1,0:T(8,128)(2,1)}, f32[2,1,16]{2,1,0:T(1,128)}) custom-call(bf16[16,2,16,128]{3,2,1,0:T(8,128)(2,1)} %shard_map.95.orecv, s32[1,16]{1,0:T(1,128)} %order.1, s32[1,16]{1,0:T(1,128)} %lens.1), custom_call_target="tpu_custom_call" | custom-call | tf_op jit(solution)/shard_map/pallas_call | solution.py:446
